TPU v7x, 512 devices: a whole 4x4x16 slice. The times are simulated.
512 devices in a mesh: pool: 64 (over x, z), tensor: 8 (over y, core).
Axes of the slice: x: 4, y: 4, z: 16, core: 2. Of those that a mesh axis runs over, the one named last changes fastest.
Arguments:
- kv_pool: bfloat16 [1024, 8, 256, 256], P('pool', 'tensor'), may hold values from -6 to 6
- queries: bfloat16 [2, 64, 64, 128], P(None, 'pool', 'tensor'), may hold values from -1200 to 1200
- new_kv: bfloat16 [2, 64, 8, 256], P(None, 'pool', 'tensor'), may hold values from -6 to 6
- block_count: int32 [64], replicated, may hold values from 1 to 64, 1024 in all
- tail_gap: int32 [64], replicated, may hold values from 0 to 253
- block_place: int32 [1024], replicated, may hold values from 0 to 1023, each once
- out_weight: bfloat16 [8192, 8192], P('tensor', 'pool'), may hold values from -1 to 1
Outputs:
- projected: bfloat16 [2, 64, 8192], P(None, 'tensor', 'pool')
Inputs may be any that keep to these rules, and one draw needn't show every extreme that they name: `block_count`: every request has 1 to 64 blocks, together exactly 1024, and one request has exactly 64. `block_place`: each global block appears exactly once.
All inputs are finite; a program needn't handle non-finite values.
Results may differ from a plain program's by a relative error of at most 0.0055.
Values may be sent and summed in bfloat16 or wider, within the bound.
A program may use at most 64 MiB of HBM per device.

v0:
```python
import jax
import jax.numpy as jnp
from jax import lax
from jax.sharding import PartitionSpec as P

masked_value = -1e30


def body(kv_pool, queries, new_kv, block_count, tail_gap, block_place, out_weight):
    blocks_here = kv_pool.shape[0]
    kv_local = kv_pool.shape[1]
    block_tokens = kv_pool.shape[2]
    head_size = kv_pool.shape[3] // 2
    req_total = block_count.shape[0]
    device = lax.axis_index("pool")
    global_ids = device * blocks_here + jnp.arange(blocks_here, dtype=jnp.int32)
    all_places = jnp.arange(block_place.shape[0], dtype=jnp.int32)
    place_rank = jnp.sum(
        jnp.where(block_place[None, :] == global_ids[:, None], all_places[None, :], 0), axis=1
    )
    ends = jnp.cumsum(block_count)
    starts = ends - block_count
    request_of = jnp.sum((ends[None, :] <= place_rank[:, None]).astype(jnp.int32), axis=1)
    chosen = jnp.arange(req_total, dtype=jnp.int32)[None, :] == request_of[:, None]
    block_index = place_rank - jnp.sum(jnp.where(chosen, starts[None, :], 0), axis=1)
    contexts = block_count * block_tokens - 2 - tail_gap
    context_of = jnp.sum(jnp.where(chosen, contexts[None, :], 0), axis=1)
    q_all, kv_new = (
        lax.all_gather(queries, "pool", axis=1, tiled=True),
        lax.all_gather(new_kv, "pool", axis=1, tiled=True),
    )
    positions = (
        block_index[:, None] * block_tokens + jnp.arange(block_tokens, dtype=jnp.int32)[None, :]
    )
    new_rows = jnp.take(kv_new, request_of, axis=1)
    cache = kv_pool
    for which in range(2):
        hit = positions == (context_of + which)[:, None]
        cache = jnp.where(hit[:, None, :, None], new_rows[which][:, :, None, :], cache)
    keys = cache[..., :head_size]
    values = cache[..., head_size:]
    group = q_all.shape[2] // kv_local
    heads_here = q_all.shape[2]
    q_blocks = jnp.take(q_all, request_of, axis=1).reshape(
        2, blocks_here, kv_local, group, head_size
    )
    scores = jnp.einsum(
        "sbkgd,bktd->sbkgt", q_blocks, keys, preferred_element_type=jnp.float32
    ) * head_size ** (-0.5)
    usable = (
        positions[None, :, :]
        <= (context_of[None, :] + jnp.arange(2, dtype=jnp.int32)[:, None])[:, :, None]
    )
    scores = jnp.where(usable[:, :, None, None, :], scores, masked_value)
    block_max = jnp.max(scores, axis=-1)
    weights = jnp.exp(scores - block_max[..., None])
    block_sum = jnp.sum(weights, axis=-1).reshape(2, blocks_here, heads_here)
    block_out = jnp.einsum(
        "sbkgt,bktd->sbkgd",
        weights.astype(jnp.bfloat16),
        values,
        preferred_element_type=jnp.float32,
    )
    block_out = block_out.reshape(2, blocks_here, heads_here, head_size)
    block_max = block_max.reshape(2, blocks_here, heads_here)
    req_max = jnp.max(
        jnp.where(chosen[None, :, :, None], block_max[:, :, None, :], masked_value), axis=1
    )
    rescale = jnp.exp(block_max - jnp.take(req_max, request_of, axis=1))
    member = chosen.astype(jnp.float32)
    req_sum = jnp.einsum(
        "br,sbh->srh", member, rescale * block_sum, precision=lax.Precision.HIGHEST
    )
    req_out = jnp.einsum(
        "br,sbhd->srhd", member, rescale[..., None] * block_out, precision=lax.Precision.HIGHEST
    )
    home_max, home_sum, home_out = (
        lax.all_to_all(req_max[None], "pool", split_axis=2, concat_axis=0, tiled=True),
        lax.all_to_all(req_sum[None], "pool", split_axis=2, concat_axis=0, tiled=True),
        lax.all_to_all(req_out[None], "pool", split_axis=2, concat_axis=0, tiled=True),
    )
    top = jnp.max(home_max, axis=0)
    factor = jnp.exp(home_max - top[None])
    total = jnp.sum(factor * home_sum, axis=0)
    combined = jnp.sum(factor[..., None] * home_out, axis=0)
    owned = combined.shape[1]
    attended = (
        (combined / total[..., None]).astype(jnp.bfloat16).reshape(2, owned, heads_here * head_size)
    )
    partial_out = jnp.einsum(
        "srk,kd->srd",
        lax.all_gather(attended, "pool", axis=1, tiled=True),
        out_weight,
        preferred_element_type=jnp.float32,
    )
    return lax.psum_scatter(partial_out, "tensor", scatter_dimension=1, tiled=True).astype(
        jnp.bfloat16
    )


def solution(mesh):
    placed = (
        P("pool", "tensor", None, None),
        P(None, "pool", "tensor", None),
        P(None, "pool", "tensor", None),
        P(),
        P(),
        P(),
        P("tensor", "pool"),
    )
    return jax.shard_map(
        body, mesh=mesh, in_specs=placed, out_specs=P(None, "tensor", "pool"), check_vma=False
    )
```

profile of v0, /device:TPU:1, one launch (start us, length us, event | category | flops | bytes accessed | tf_op | source)
XLA Modules:
  0.0 394.3 jit_solution(2281413403503197094)
XLA Ops:
  6.5 0.8 copy.38
  7.5 0.9 select_reduce_fusion.1
  8.7 0.7 add_subtract_fusion
  9.8 69.9 %all_gather.9 = bf16[2,64,1,256]{3,0,2,1:T(2,128)(2,1)S(1)} all-gather(bf16[2,1,1,256]{3,0,2,1:T(2,128)(2,1)} %param.9), channel_id=1, replica_groups=mesh['pool'=64,'tensor'=8] {'pool'}, dimensions={1}, use_global_device_ids=true | all-gather | bytes 66560 | tf_op jit(solution)/shard_map/all_gather | solution.py:30
  79.7 0.6 gather_fusion
  80.4 73.0 %all_gather.10 = bf16[2,64,8,128]{3,2,1,0:T(8,128)(2,1)S(1)} all-gather(bf16[2,1,8,128]{3,2,1,0:T(8,128)(2,1)} %param.8), channel_id=1, replica_groups=mesh['pool'=64,'tensor'=8] {'pool'}, dimensions={1}, use_global_device_ids=true | all-gather | bytes 266240 | tf_op jit(solution)/shard_map/all_gather | solution.py:29
  153.4 0.6 gather_fusion.1
  154.1 3.2 fusion
  157.3 0.5 fusion.36
  157.9 0.7 copy.41
  158.6 9.0 %all-to-all-start = ((f32[1,2,64,8]{3,1,0,2:T(2,128)}), f32[1,2,64,8]{3,1,0,2:T(2,128)S(1)}, u32[]{:S(2)}, u32[]{:S(2)}) async-start(f32[1,2,64,8]{3,1,0,2:T(2,128)} %copy.41), calls=%async_computation | async-start | bytes 131072 | tf_op jit(solution)/shard_map/all_to_all | solution.py:78
  168.0 0.6 gather_fusion.2
  169.2 0.7 copy.46
  169.9 11.4 %all-to-all-done = f32[1,2,64,8]{3,1,0,2:T(2,128)S(1)} async-done(((f32[1,2,64,8]{3,1,0,2:T(2,128)}), f32[1,2,64,8]{3,1,0,2:T(2,128)S(1)}, u32[]{:S(2)}, u32[]{:S(2)}) %all-to-all-start) | async-done | bytes 4128 | tf_op jit(solution)/shard_map/all_to_all | solution.py:78
  181.3 4.6 %all-to-all-start.2 = ((f32[1,2,64,8]{3,1,0,2:T(2,128)}), f32[1,2,64,8]{3,1,0,2:T(2,128)S(1)}, u32[]{:S(2)}, u32[]{:S(2)}) async-start(f32[1,2,64,8]{3,1,0,2:T(2,128)} %copy.46), calls=%async_computation.2 | async-start | bytes 131072 | tf_op jit(solution)/shard_map/all_to_all | solution.py:79
  185.9 0.5 convolution_bitcast_fusion
  186.4 1.1 copy.44
  187.5 11.9 %all-to-all-done.2 = f32[1,2,64,8]{3,1,0,2:T(2,128)S(1)} async-done(((f32[1,2,64,8]{3,1,0,2:T(2,128)}), f32[1,2,64,8]{3,1,0,2:T(2,128)S(1)}, u32[]{:S(2)}, u32[]{:S(2)}) %all-to-all-start.2) | async-done | bytes 4128 | tf_op jit(solution)/shard_map/all_to_all | solution.py:79
  199.5 4.6 %all-to-all-start.1 = ((f32[1,2,64,8,128]{4,3,1,0,2:T(8,128)}), f32[1,2,64,8,128]{4,3,1,0,2:T(8,128)S(1)}, u32[]{:S(2)}, u32[]{:S(2)}) async-start(f32[1,2,64,8,128]{4,3,1,0,2:T(8,128)} %copy.44), calls=%async_computation.1 | async-start | bytes 1048576 | tf_op jit(solution)/shard_map/all_to_all | solution.py:80
  204.4 20.5 %all-to-all-done.1 = f32[1,2,64,8,128]{4,3,1,0,2:T(8,128)S(1)} async-done(((f32[1,2,64,8,128]{4,3,1,0,2:T(8,128)}), f32[1,2,64,8,128]{4,3,1,0,2:T(8,128)S(1)}, u32[]{:S(2)}, u32[]{:S(2)}) %all-to-all-start.1) | async-done | bytes 524320 | tf_op jit(solution)/shard_map/all_to_all | solution.py:80
  225.2 66.4 %all_gather.11 = bf16[2,64,1024]{2,0,1:T(2,128)(2,1)S(1)} all-gather(bf16[2,1,1024]{2,0,1:T(2,128)(2,1)S(1)} %convert_element_type.28), channel_id=1, replica_groups=mesh['pool'=64,'tensor'=8] {'pool'}, dimensions={1}, use_global_device_ids=true | all-gather | bytes 266240 | tf_op jit(solution)/shard_map/all_gather | solution.py:92
  291.6 0.8 fusion.5
  292.5 93.7 %reduce-scatter.2.cloned.1.call-done = f32[2,8,128]{2,1,0:T(8,128)} async-done(((f32[2,64,128]{2,1,0:T(8,128)}), f32[2,8,128]{2,1,0:T(8,128)}) %reduce-scatter.2.cloned.1.call-update) | async-done | bytes 8208 | tf_op jit(solution)/shard_map/reduce_scatter | solution.py:96
  386.1 1.3 convert_element_type.29
  (34 shorter events, 2.7 us)
Async XLA Ops:
  6.5 285.1 %copy-start = (bf16[1024,128]{1,0:T(8,128)(2,1)S(1)}, bf16[1024,128]{1,0:T(8,128)(2,1)}, u32[]{:S(2)}) copy-start(bf16[1024,128]{1,0:T(8,128)(2,1)} %param.13) | copy-start | bytes 786436
  158.6 22.7 %all-to-all-start = ((f32[1,2,64,8]{3,1,0,2:T(2,128)}), f32[1,2,64,8]{3,1,0,2:T(2,128)S(1)}, u32[]{:S(2)}, u32[]{:S(2)}) async-start(f32[1,2,64,8]{3,1,0,2:T(2,128)} %copy.41), calls=%async_computation | async-start | bytes 131072 | tf_op jit(solution)/shard_map/all_to_all | solution.py:78
  181.3 18.1 %all-to-all-start.2 = ((f32[1,2,64,8]{3,1,0,2:T(2,128)}), f32[1,2,64,8]{3,1,0,2:T(2,128)S(1)}, u32[]{:S(2)}, u32[]{:S(2)}) async-start(f32[1,2,64,8]{3,1,0,2:T(2,128)} %copy.46), calls=%async_computation.2 | async-start | bytes 131072 | tf_op jit(solution)/shard_map/all_to_all | solution.py:79
  199.5 25.4 %all-to-all-start.1 = ((f32[1,2,64,8,128]{4,3,1,0,2:T(8,128)}), f32[1,2,64,8,128]{4,3,1,0,2:T(8,128)S(1)}, u32[]{:S(2)}, u32[]{:S(2)}) async-start(f32[1,2,64,8,128]{4,3,1,0,2:T(8,128)} %copy.44), calls=%async_computation.1 | async-start | bytes 1048576 | tf_op jit(solution)/shard_map/all_to_all | solution.py:80
  204.1 182.0 %reduce-scatter.2.cloned.1.call-start = ((), (), s32[]{:S(2)}) async-start(), calls=%async_computation.4 | async-start | bytes 73728 | tf_op jit(solution)/shard_map/reduce_scatter | solution.py:96
Sparse Core Ops, SparseCore 0:
  292.6 93.5 reduce-scatter.1
where the time goes:
time: 396 us; the launch traced here: 394 us
  blocking collectives  209 us (53%)
  waiting for transfers between devices  138 us (35%)
  starting transfers between devices  18.3 us (5%)
  between operations  13.5 us (3%)
  other arithmetic  8.01 us (2%)
  local copies, waits for them, and re-layouts  5.27 us (1%)
    reduce_scatter x1, waiting for transfers between devices, body(): lax.psum_scatter(partial_out, 'tensor', scatter_dimension=1, tiled=True)  93.7 us
    all_gather x1, blocking collectives, body(): lax.all_gather(queries, 'pool', axis=1, tiled=True)  73 us
    all_gather x1, blocking collectives, body(): lax.all_gather(new_kv, 'pool', axis=1, tiled=True)  69.9 us
    all_gather x1, blocking collectives, body(): lax.all_gather(attended, 'pool', axis=1, tiled=True)  66.4 us
    all_to_all x1, waiting for transfers between devices, body(): lax.all_to_all(req_out[None], 'pool', split_axis=2, concat_axis=0, tiled=...  20.5 us
    all_to_all x1, waiting for transfers between devices, body(): lax.all_to_all(req_sum[None], 'pool', split_axis=2, concat_axis=0, tiled=...  11.9 us
    all_to_all x1, waiting for transfers between devices, body(): lax.all_to_all(req_max[None], 'pool', split_axis=2, concat_axis=0, tiled=...  11.4 us
    all_to_all x1, starting transfers between devices, body(): lax.all_to_all(req_max[None], 'pool', split_axis=2, concat_axis=0, tiled=...  9.01 us
  transfers between devices with their start and end apart: 4, of which 4 were waited for; matrix products, arithmetic and copies ran while one was open for 1% of the time, Pallas kernels for 0%

commit v1 on v0

v1 whole, which is shorter than its diff:
```python
import functools

import jax
import jax.numpy as jnp
from jax import lax
from jax.experimental import pallas as pl
from jax.experimental.pallas import tpu as pltpu
from jax.sharding import PartitionSpec as P

MESH = pl.DeviceIdType.MESH
masked_value = -1e30
groups = 4


def iota(shape, axis):
    return lax.broadcasted_iota(jnp.int32, shape, axis).astype(jnp.float32)


def block_tables(bp, cnt, gap, ids, tokens):
    reqs = cnt.shape[1]
    blocks = ids.shape[0]
    rank = jnp.sum(jnp.where(bp == ids, iota((blocks, bp.shape[1]), 1), 0.0), axis=1, keepdims=True)
    row, col = iota((reqs, reqs), 0), iota((reqs, reqs), 1)
    cnt_col = jnp.sum(jnp.where(row == col, cnt, 0.0), axis=1, keepdims=True)
    ends = jnp.sum(jnp.where(row <= col, cnt_col, 0.0), axis=0, keepdims=True)
    request = jnp.sum(jnp.where(ends <= rank, 1.0, 0.0), axis=1, keepdims=True)
    offset = cnt * tokens - 2.0 - gap + (ends - cnt) * tokens
    picked = jnp.sum(
        jnp.where(iota((blocks, reqs), 1) == request, offset, 0.0), axis=1, keepdims=True
    )
    return request, picked - rank * tokens


def kernel(
    X, Z, T,
    q_ref, nk_ref, cnt_ref, gap_ref, bp_ref, kv_hbm, w_hbm, out_ref,
    kv, w, qbuf, obuf, lbuf, oz, lz, ob, lb, abuf, att, ysend, fin,
    sem_in, s1, r1, s2, r2, sa, ra, sal, ral, sb, rb, sbl, rbl, sc, rc, sd, rd, se, re,
):
    pool, ten = lax.axis_index("pool"), lax.axis_index("tensor")
    x, z = lax.div(pool, Z), lax.rem(pool, Z)
    blocks, tokens, hd2 = kv.shape
    hd = hd2 // 2
    rows = q_ref.shape[0]
    reqs = cnt_ref.shape[1]
    per_t = reqs // T
    t_per_x = Z // per_t
    heads = rows // 2
    gs = Z // groups
    scale = hd ** (-0.5)

    def along_z(o):
        return (x * Z + lax.rem(z + o, Z), ten)

    def along_x(o):
        return (lax.rem(x + o, X) * Z + z, ten)

    def loop(low, high, body):
        def step(i, carry):
            body(i)
            return carry

        lax.fori_loop(low, high, step, 0)

    def remote(src, dst, send, recv, device):
        return pltpu.make_async_remote_copy(
            src_ref=src, dst_ref=dst, send_sem=send, recv_sem=recv,
            device_id=device, device_id_type=MESH,
        )

    kv_in = pltpu.make_async_copy(kv_hbm, kv, sem_in.at[0])
    w_in = pltpu.make_async_copy(w_hbm, w, sem_in.at[1])
    kv_in.start()
    w_in.start()

    barrier = pltpu.get_barrier_semaphore()

    def greet(device):
        pl.semaphore_signal(barrier, inc=1, device_id=device, device_id_type=MESH)

    loop(1, Z, lambda o: greet(along_z(o)))
    loop(1, X, lambda o: greet(along_x(o)))
    loop(1, T, lambda o: greet((pool, lax.rem(ten + o, T))))
    qbuf[pool] = q_ref[...]
    pl.semaphore_wait(barrier, Z + X + T - 3)

    def z_copy(buf, s, r, o):
        return remote(buf.at[pool], buf.at[pool], s.at[o], r.at[z], along_z(o))

    def z_arrival(buf, s, r, at):
        here = buf.at[x * Z + at]
        return remote(here, here, s.at[0], r.at[at], along_z(1))

    def x_copy(buf, s, r, g, o):
        part = buf.at[pl.ds(x * Z + g * gs, gs)]
        return remote(part, part, s.at[g, o], r.at[g, x], along_x(o))

    def x_arrival(buf, s, r, g, from_x):
        part = buf.at[pl.ds(from_x * Z + g * gs, gs)]
        return remote(part, part, s.at[g, 0], r.at[g, from_x], along_x(1))

    def gather_z(buf, s, r):
        loop(1, Z, lambda o: z_copy(buf, s, r, o).start())

    def gather_x(buf, sz, rz, sx, rx):
        for turn in (0, 1, 3, 2):
            g = lax.rem(lax.div(z, gs) + turn, groups)

            def arrive(i):
                at = g * gs + i

                @pl.when(at != z)
                def _():
                    z_arrival(buf, sz, rz, at).wait_recv()

            loop(0, gs, arrive)
            loop(1, X, lambda o: x_copy(buf, sx, rx, g, o).start())

    def gathered(buf, sx, rx, from_x):
        loop(0, groups, lambda g: x_arrival(buf, sx, rx, g, from_x).wait_recv())

    def gather_sent(buf, sz, rz, sx, rx):
        loop(1, Z, lambda o: z_copy(buf, sz, rz, o).wait_send())
        loop(0, groups, lambda g: loop(1, X, lambda o: x_copy(buf, sx, rx, g, o).wait_send()))

    gather_z(qbuf, s1, r1)

    cnt = cnt_ref[...].astype(jnp.float32)
    gap = gap_ref[...].astype(jnp.float32)
    line = X * blocks
    b = lax.broadcasted_iota(jnp.int32, (line, 1), 0)
    ids = (lax.rem(x + lax.div(b, blocks), X) * Z + z) * blocks + lax.rem(b, blocks)
    request, usable = block_tables(bp_ref[...], cnt, gap, ids, float(tokens))
    own_request, own_usable = request[:blocks], usable[:blocks]

    own_rows = blocks * rows
    picked_row = (
        jnp.broadcast_to((own_request * rows)[:, None, :], (blocks, rows, 1))
        + iota((blocks, rows, 1), 1)
    ).reshape(own_rows, 1)
    lane = iota((own_rows, Z * rows), 1)

    def pick(j):
        first = lax.rem(x + j, X) * (Z * rows)
        return jnp.where(picked_row - first.astype(jnp.float32) == lane, 1.0, 0.0).astype(
            jnp.bfloat16
        )

    picks = [pick(j) for j in range(X)]

    local = request - (x * Z).astype(jnp.float32)
    line_rows = line * rows
    wide = lax.broadcasted_iota(jnp.int32, (line, line_rows), 1)
    local_lane = jnp.sum(
        jnp.where(
            lax.broadcasted_iota(jnp.int32, (line, line_rows), 0) == lax.div(wide, rows),
            local, 0.0,
        ),
        axis=0, keepdims=True,
    )
    goes_to = local_lane * rows + lax.rem(
        lax.broadcasted_iota(jnp.int32, (1, line_rows), 1), rows
    ).astype(jnp.float32)
    merge = jnp.where(iota((Z * rows, line_rows), 0) == goes_to, 1.0, 0.0).astype(jnp.bfloat16)

    q_own = q_ref[...].astype(jnp.float32)
    new = nk_ref[...].astype(jnp.float32)
    score0 = jnp.sum(q_own * new[0:1, :hd], axis=1, keepdims=True) * scale
    score1 = jnp.sum(q_own * new[1:2, :hd], axis=1, keepdims=True) * scale
    score1 = jnp.where(iota((rows, 1), 0) >= heads, score1, masked_value)
    new_max = jnp.maximum(score0, score1)
    weight0, weight1 = jnp.exp(score0 - new_max), jnp.exp(score1 - new_max)
    new_sum = weight0 + weight1
    new_out = (
        weight0.astype(jnp.bfloat16).astype(jnp.float32) * new[0:1, hd:]
        + weight1.astype(jnp.bfloat16).astype(jnp.float32) * new[1:2, hd:]
    ) / new_sum
    new_lse = new_max + jnp.log(new_sum)

    gather_x(qbuf, s1, r1, s2, r2)

    def dot(a, c):
        return jnp.dot(a, c, preferred_element_type=jnp.float32)

    def column(j):
        from_x = lax.rem(x + j, X)
        if j:
            gathered(qbuf, s2, r2, from_x)
        return qbuf[pl.ds(from_x * Z, Z)].reshape(Z * rows, hd)

    q_sel = dot(picks[0], column(0))
    for j in range(1, X):
        q_sel += dot(picks[j], column(j))
    q_sel = q_sel.astype(jnp.bfloat16).reshape(blocks, rows, hd)

    kv_in.wait()

    def o_copy(c, o):
        part = pl.ds(c * step, step)
        return remote(
            obuf.at[0, part], obuf.at[X - o, part], sa.at[c, o], ra.at[c, X - o], along_x(o)
        )

    def l_copy(o):
        return remote(lbuf.at[0], lbuf.at[X - o], sal.at[o], ral.at[X - o], along_x(o))

    step = blocks // 4
    spread = lax.rem(lax.broadcasted_iota(jnp.int32, (step, rows, 128), 2), rows)
    spread = spread == lax.broadcasted_iota(jnp.int32, (step, rows, 128), 1)
    position = iota((step, rows, tokens), 2)
    lses = []
    for c in range(4):
        part = slice(c * step, (c + 1) * step)
        keys = kv[part, :, :hd]
        values = kv[part, :, hd:]
        scores = jnp.einsum(
            "bqd,btd->bqt", q_sel[part], keys, preferred_element_type=jnp.float32
        ) * scale
        limit = jnp.broadcast_to(own_usable[part][:, None, :], (step, rows, 1))
        scores = jnp.where(position < limit, scores, masked_value)
        top = jnp.max(scores, axis=2, keepdims=True)
        weights = jnp.exp(scores - top)
        total = jnp.sum(weights, axis=2, keepdims=True)
        out = jnp.einsum(
            "bqt,btd->bqd", weights.astype(jnp.bfloat16), values,
            preferred_element_type=jnp.float32,
        )
        obuf[0, part] = (out / total).astype(jnp.bfloat16)
        loop(1, X, lambda o: o_copy(c, o).start())
        lses.append(jnp.sum(jnp.where(spread, top + jnp.log(total), 0.0), axis=1))
    lbuf[0] = jnp.concatenate(lses, axis=0)
    loop(1, X, lambda o: l_copy(o).start())

    for j in range(1, X):
        l_here = lbuf.at[j]
        remote(l_here, l_here, sal.at[0], ral.at[j], along_x(1)).wait_recv()
    lse = lbuf[...].reshape(line, 128)
    where_to = jnp.broadcast_to(local, (line, 128))
    tops = []
    top_of = jnp.zeros((line, 128), jnp.float32)
    for i in range(Z):
        mine = where_to == float(i)
        tops.append(jnp.max(jnp.where(mine, lse, masked_value), axis=0, keepdims=True))
        top_of = jnp.where(mine, tops[i], top_of)
    inside = jnp.logical_and(where_to >= 0.0, where_to < float(Z))
    factor = jnp.where(inside, jnp.exp(jnp.where(inside, lse - top_of, 0.0)), 0.0)
    sum_of = jnp.ones((line, 128), jnp.float32)
    for i in range(Z):
        mine = where_to == float(i)
        total = jnp.sum(jnp.where(mine, factor, 0.0), axis=0, keepdims=True)
        sum_of = jnp.where(mine, total, sum_of)
        lz[i] = jnp.where(
            total > 0.0, tops[i] + jnp.log(jnp.where(total > 0.0, total, 1.0)), masked_value
        )
    factor = factor / sum_of

    def to_column(values, count):
        shape = (count, rows, 128)
        diagonal = lax.broadcasted_iota(jnp.int32, shape, 2) == lax.broadcasted_iota(
            jnp.int32, shape, 1
        )
        return jnp.sum(
            jnp.where(diagonal, jnp.broadcast_to(values, shape), 0.0), axis=2, keepdims=True
        )

    factor = to_column(factor[:, None, :], line)
    for j in range(1, X):
        for c in range(4):
            o_here = obuf.at[j, pl.ds(c * step, step)]
            remote(o_here, o_here, sa.at[c, 0], ra.at[c, j], along_x(1)).wait_recv()
    scaled = (obuf[...].reshape(line, rows, hd).astype(jnp.float32) * factor).reshape(
        line_rows, hd
    )
    high = scaled.astype(jnp.bfloat16)
    low = (scaled - high.astype(jnp.float32)).astype(jnp.bfloat16)
    merged = dot(merge, high) + dot(merge, low)
    oz[...] = merged.astype(jnp.bfloat16).reshape(Z, rows, hd)

    def oz_copy(o):
        to = lax.rem(z + o, Z)
        return remote(oz.at[to], ob.at[Z - o], sb.at[o], rb.at[Z - o], along_z(o))

    def lz_copy(o):
        to = lax.rem(z + o, Z)
        return remote(lz.at[to], lb.at[Z - o], sbl.at[o], rbl.at[Z - o], along_z(o))

    def send_z(o):
        oz_copy(o).start()
        lz_copy(o).start()

    loop(1, Z, send_z)
    ob[0] = oz[z]
    lb[0] = lz[z]

    def arrive_z(o):
        o_here, l_here = ob.at[o], lb.at[o]
        remote(o_here, o_here, sb.at[0], rb.at[o], along_z(1)).wait_recv()
        remote(l_here, l_here, sbl.at[0], rbl.at[o], along_z(1)).wait_recv()

    loop(1, Z, arrive_z)
    lse = to_column(lb[...], Z)
    top = jnp.maximum(jnp.max(lse, axis=0), new_lse)
    factor = jnp.exp(lse - top[None])
    new_factor = jnp.exp(new_lse - top)
    total = jnp.sum(factor, axis=0) + new_factor
    combined = jnp.sum(factor * ob[...].astype(jnp.float32), axis=0) + new_factor * new_out
    abuf[pool] = (combined / total).astype(jnp.bfloat16)

    gather_z(abuf, sc, rc)
    w_in.wait()
    gather_x(abuf, sc, rc, sd, rd)

    def y_copy(j, u, to):
        return remote(
            ysend.at[j, :, pl.ds(u * per_t, per_t)], fin.at[ten], se.at[j, u], re.at[ten],
            (pool, to),
        )

    for j in range(X):
        from_x = lax.rem(x + j, X)
        if j:
            gathered(abuf, sd, rd, from_x)
        att[...] = abuf[pl.ds(from_x * Z, Z)].astype(jnp.float32).reshape(Z * rows, hd)
        steps = []
        for s in range(2):
            parts = [att[pl.ds(s * heads + h, Z, stride=rows), :] for h in range(heads)]
            steps.append(jnp.concatenate(parts, axis=1))
        a = jnp.concatenate(steps, axis=0).astype(jnp.bfloat16)
        ysend[j] = dot(a, w[...]).reshape(2, Z, w.shape[1])
        for u in range(t_per_x):
            to = from_x * t_per_x + u

            @pl.when(to != ten)
            def _():
                y_copy(j, u, to).start()

            @pl.when(to == ten)
            def _():
                fin[ten] = ysend[j, :, u * per_t : (u + 1) * per_t]

    def y_arrive(o):
        at = lax.rem(ten + o, T)
        here = fin.at[at]
        remote(here, here, se.at[0, 0], re.at[at], (pool, at)).wait_recv()

    loop(1, T, y_arrive)
    out_ref[...] = jnp.sum(fin[...], axis=0).astype(jnp.bfloat16)

    gather_sent(qbuf, s1, r1, s2, r2)
    for c in range(4):
        loop(1, X, lambda o: o_copy(c, o).wait_send())
    loop(1, X, lambda o: l_copy(o).wait_send())
    loop(1, Z, lambda o: oz_copy(o).wait_send())
    loop(1, Z, lambda o: lz_copy(o).wait_send())
    gather_sent(abuf, sc, rc, sd, rd)
    for j in range(X):
        for u in range(t_per_x):
            to = lax.rem(x + j, X) * t_per_x + u

            @pl.when(to != ten)
            def _():
                y_copy(j, u, to).wait_send()


def body(X, Z, T, kv_pool, queries, new_kv, block_count, tail_gap, block_place, out_weight):
    blocks, _, tokens, hd2 = kv_pool.shape
    hd = hd2 // 2
    rows = 2 * queries.shape[2]
    reqs = block_count.shape[0]
    columns = out_weight.shape[1]
    pools = X * Z
    dma = pltpu.SemaphoreType.DMA
    in_vmem = pl.BlockSpec(memory_space=pltpu.VMEM)
    in_any = pl.BlockSpec(memory_space=pl.ANY)
    return pl.pallas_call(
        functools.partial(kernel, X, Z, T),
        out_shape=jax.ShapeDtypeStruct((2, reqs // T, columns), jnp.bfloat16),
        in_specs=[in_vmem] * 5 + [in_any] * 2,
        out_specs=in_vmem,
        scratch_shapes=[
            pltpu.VMEM((blocks, tokens, hd2), jnp.bfloat16),
            pltpu.VMEM(out_weight.shape, jnp.bfloat16),
            pltpu.VMEM((pools, rows, hd), jnp.bfloat16),
            pltpu.VMEM((X, blocks, rows, hd), jnp.bfloat16),
            pltpu.VMEM((X, blocks, 128), jnp.float32),
            pltpu.VMEM((Z, rows, hd), jnp.bfloat16),
            pltpu.VMEM((Z, 1, 128), jnp.float32),
            pltpu.VMEM((Z, rows, hd), jnp.bfloat16),
            pltpu.VMEM((Z, 1, 128), jnp.float32),
            pltpu.VMEM((pools, rows, hd), jnp.bfloat16),
            pltpu.VMEM((Z * rows, hd), jnp.float32),
            pltpu.VMEM((X, 2, Z, columns), jnp.float32),
            pltpu.VMEM((T, 2, reqs // T, columns), jnp.float32),
            dma((2,)),
            dma((Z,)), dma((Z,)),
            dma((groups, X)), dma((groups, X)),
            dma((4, X)), dma((4, X)), dma((X,)), dma((X,)),
            dma((Z,)), dma((Z,)), dma((Z,)), dma((Z,)),
            dma((Z,)), dma((Z,)),
            dma((groups, X)), dma((groups, X)),
            dma((X, Z * T // reqs)), dma((T,)),
        ],
        compiler_params=pltpu.CompilerParams(
            collective_id=0, has_side_effects=True, vmem_limit_bytes=40 * 1024 * 1024
        ),
    )(
        queries.reshape(rows, hd),
        new_kv.reshape(2, hd2),
        block_count.reshape(1, reqs),
        tail_gap.reshape(1, reqs),
        block_place.reshape(1, block_place.shape[0]),
        kv_pool.reshape(blocks, tokens, hd2),
        out_weight,
    )


def solution(mesh):
    pools, tensors = mesh.shape["pool"], mesh.shape["tensor"]
    Z = 16 if pools == 64 else 4
    placed = (
        P("pool", "tensor", None, None),
        P(None, "pool", "tensor", None),
        P(None, "pool", "tensor", None),
        P(),
        P(),
        P(),
        P("tensor", "pool"),
    )
    return jax.shard_map(
        functools.partial(body, pools // Z, Z, tensors),
        mesh=mesh, in_specs=placed, out_specs=P(None, "tensor", "pool"), check_vma=False,
    )
```

time: 396 us -> 66.1 us (0.17)
  the two profiles are of different devices: /device:TPU:1 before, /device:TPU:3 now
where the time goes in v1:
time: 66.1 us; the launch traced here: 65.8 us
  Pallas kernels  59.3 us (90%)
  local copies, waits for them, and re-layouts  6.5 us (10%)
    pallas_call x1, Pallas kernels, body(): pl.pallas_call(functools.partial(kernel, X, Z, T), out_shape=jax.ShapeDty...  59.3 us
    unnamed x15, local copies, waits for them, and re-layouts  6.5 us

profile of v1, /device:TPU:3, one launch (start us, length us, event | category | flops | bytes accessed | tf_op | source)
XLA Modules:
  0.0 65.8 jit_solution(7457690877095110505)
XLA Ops:
  0.0 0.0 copy-start
  0.0 1.6 %copy-done = bf16[16,1,256,256]{3,2,1,0:T(8,128)(2,1)S(1)} copy-done((bf16[16,1,256,256]{3,2,1,0:T(8,128)(2,1)S(1)}, bf16[16,1,256,256]{3,2,1,0:T(8,128)(2,1)}, u32[]{:S(2)}) %copy-start) | copy-done | bytes 2097176
  1.6 0.0 copy-start.1
  1.6 0.9 %copy-done.1 = bf16[1024,128]{1,0:T(8,128)(2,1)S(1)} copy-done((bf16[1024,128]{1,0:T(8,128)(2,1)S(1)}, bf16[1024,128]{1,0:T(8,128)(2,1)}, u32[]{:S(2)}) %copy-start.1) | copy-done | bytes 262168
  2.5 0.0 copy-start.2
  2.5 0.7 %copy-done.2 = bf16[2,1,8,128]{3,2,1,0:T(8,128)(2,1)S(1)} copy-done((bf16[2,1,8,128]{3,2,1,0:T(8,128)(2,1)S(1)}, bf16[2,1,8,128]{3,2,1,0:T(8,128)(2,1)}, u32[]{:S(2)}) %copy-start.2) | copy-done | bytes 4120
  3.2 0.0 copy-start.3
  3.2 0.7 %copy-done.3 = s32[1024]{0:T(1024)S(1)} copy-done((s32[1024]{0:T(1024)S(1)}, s32[1024]{0:T(1024)}, u32[]{:S(2)}) %copy-start.3) | copy-done | bytes 4120
  3.9 0.0 copy-start.4
  3.9 0.7 %copy-done.4 = bf16[2,1,1,256]{3,0,2,1:T(2,128)(2,1)S(1)} copy-done((bf16[2,1,1,256]{3,0,2,1:T(2,128)(2,1)S(1)}, bf16[2,1,1,256]{3,0,2,1:T(2,128)(2,1)}, u32[]{:S(2)}) %copy-start.4) | copy-done | bytes 1048
  4.6 0.0 copy-start.5
  4.6 0.7 copy-done.5
  5.3 0.0 copy-start.6
  5.3 0.7 copy-done.6
  5.9 59.3 %shard_map.73 = bf16[2,8,128]{2,1,0:T(8,128)(2,1)S(1)} custom-call(bf16[16,128]{1,0:T(8,128)(2,1)S(1)} %bitcast.7, bf16[2,256]{1,0:T(2,128)(2,1)S(1)} %bitcast.9, s32[1,64]{1,0:T(1,128)S(1)} %bitcast.10, s32[1,64]{1,0:T(1,128)S(1)} %bitcast.11, s32[1,1024]{1,0:T(1,128)S(1)} %bitcast.8, bf16[16,256,256]{2,1,0:T(8,128)(2,1)S(1)} %bitcast.6, ...), custom_call_target="tpu_custom_call" | custom-call | tf_op jit(solution)/shard_map/pallas_call | solution.py:375
  65.2 0.6 copy.9
Async XLA Ops:
  0.0 1.6 %copy-start = (bf16[16,1,256,256]{3,2,1,0:T(8,128)(2,1)S(1)}, bf16[16,1,256,256]{3,2,1,0:T(8,128)(2,1)}, u32[]{:S(2)}) copy-start(bf16[16,1,256,256]{3,2,1,0:T(8,128)(2,1)} %param.7) | copy-start | bytes 6291460
  1.6 0.9 %copy-start.1 = (bf16[1024,128]{1,0:T(8,128)(2,1)S(1)}, bf16[1024,128]{1,0:T(8,128)(2,1)}, u32[]{:S(2)}) copy-start(bf16[1024,128]{1,0:T(8,128)(2,1)} %w_hbm.1) | copy-start | bytes 786436
  2.5 0.7 %copy-start.2 = (bf16[2,1,8,128]{3,2,1,0:T(8,128)(2,1)S(1)}, bf16[2,1,8,128]{3,2,1,0:T(8,128)(2,1)}, u32[]{:S(2)}) copy-start(bf16[2,1,8,128]{3,2,1,0:T(8,128)(2,1)} %param.8) | copy-start | bytes 12292
  3.2 0.7 %copy-start.3 = (s32[1024]{0:T(1024)S(1)}, s32[1024]{0:T(1024)}, u32[]{:S(2)}) copy-start(s32[1024]{0:T(1024)} %param.12) | copy-start | bytes 12292
  3.9 0.7 %copy-start.4 = (bf16[2,1,1,256]{3,0,2,1:T(2,128)(2,1)S(1)}, bf16[2,1,1,256]{3,0,2,1:T(2,128)(2,1)}, u32[]{:S(2)}) copy-start(bf16[2,1,1,256]{3,0,2,1:T(2,128)(2,1)} %param.9) | copy-start | bytes 3076
  4.6 0.7 copy-start.5
  5.3 0.7 copy-start.6

commit v2 on v0

v2 whole, which is shorter than its diff:
```python
import functools

import jax
import jax.numpy as jnp
from jax import lax
from jax.experimental import pallas as pl
from jax.experimental.pallas import tpu as pltpu
from jax.sharding import PartitionSpec as P

MESH = pl.DeviceIdType.MESH
masked_value = -1e30
N = 4
chunks = 4


def iota(shape, axis):
    return lax.broadcasted_iota(jnp.int32, shape, axis)


def reals(shape, axis):
    return iota(shape, axis).astype(jnp.float32)


def block_tables(bp, cnt, gap, ids, tokens):
    reqs = cnt.shape[1]
    blocks = ids.shape[0]
    rank = jnp.sum(jnp.where(bp == ids, reals((blocks, bp.shape[1]), 1), 0.0), axis=1, keepdims=True)
    row, col = iota((reqs, reqs), 0), iota((reqs, reqs), 1)
    cnt_col = jnp.sum(jnp.where(row == col, cnt, 0.0), axis=1, keepdims=True)
    ends = jnp.sum(jnp.where(row <= col, cnt_col, 0.0), axis=0, keepdims=True)
    request = jnp.sum(jnp.where(ends <= rank, 1.0, 0.0), axis=1, keepdims=True)
    offset = cnt * tokens - 2.0 - gap + (ends - cnt) * tokens
    picked = jnp.sum(
        jnp.where(reals((blocks, reqs), 1) == request, offset, 0.0), axis=1, keepdims=True
    )
    return request, picked - rank * tokens


def to_column(values, count, rows):
    shape = (count, rows, 128)
    return jnp.sum(
        jnp.where(iota(shape, 2) == iota(shape, 1), jnp.broadcast_to(values, shape), 0.0),
        axis=2, keepdims=True,
    )


def kernel(
    X, Z, T,
    q_hbm, nk_hbm, cnt_hbm, gap_hbm, bp_hbm, kv_hbm, w_hbm, out_ref,
    q_ref, nk_ref, cnt_ref, gap_ref, bp_ref, kv, w,
    qbuf, pick_ref, put_ref, pbuf, lz, rbuf, rl, fb, fl, abuf, att, ysend, fin,
    sem_in, sf, rf, sp, rp, so, ro, sl, rls, sfo, rfo, sfl, rfl, sg, rg, se, re,
):
    pool, ten = lax.axis_index("pool"), lax.axis_index("tensor")
    x, z = lax.div(pool, Z), lax.rem(pool, Z)
    F = Z // N
    G = X * N
    n, f = lax.rem(z, N), lax.div(z, N)
    blocks, tokens, hd2 = kv.shape
    hd = hd2 // 2
    rows = q_ref.shape[0]
    reqs = cnt_ref.shape[1]
    per_t = reqs // T
    t_per_x = Z // per_t
    heads = rows // 2
    scale = hd ** (-0.5)
    frows = F * rows

    xs = [x] + [lax.rem(x + j, X) for j in range(1, X)]
    hops = [0, 1, 2, Z - 1]
    zs = [z] + [lax.rem(z + hops[j], Z) for j in range(1, N)]
    far = [(x * Z + lax.rem(z + N * j, Z), ten) for j in range(F)]
    near = [(xs[g // N] * Z + zs[g % N], ten) for g in range(G)]
    sides = [(pool, lax.rem(ten + j, T)) for j in range(T)]

    def back(g):
        return ((X - g // N) % X) * N + (N - g % N) % N

    order = sorted(range(1, G), key=lambda g: -(min(g // N, X - g // N) + [0, 1, 2, 1][g % N]))

    def remote(src, dst, send, recv, device):
        return pltpu.make_async_remote_copy(
            src_ref=src, dst_ref=dst, send_sem=send, recv_sem=recv,
            device_id=device, device_id_type=MESH,
        )

    def arrived(dst, recv, send):
        remote(dst, dst, send, recv, far[1]).wait_recv()

    pairs = [
        (q_hbm, q_ref), (bp_hbm, bp_ref), (cnt_hbm, cnt_ref), (gap_hbm, gap_ref),
        (nk_hbm, nk_ref), (kv_hbm, kv), (w_hbm, w),
    ]
    loads = [pltpu.make_async_copy(a, b, sem_in.at[i]) for i, (a, b) in enumerate(pairs)]
    for load in loads:
        load.start()

    barrier = pltpu.get_barrier_semaphore()
    for device in far[1:] + near[1:] + sides[1:]:
        pl.semaphore_signal(barrier, inc=1, device_id=device, device_id_type=MESH)
    loads[0].wait()
    qbuf[0, f] = q_ref[...]
    pl.semaphore_wait(barrier, F + G + T - 3)

    def q_far(j):
        return remote(qbuf.at[0, f], qbuf.at[0, f], sf.at[j], rf.at[f], far[j])

    def q_near(g):
        return remote(qbuf.at[0], qbuf.at[back(g)], sp.at[g], rp.at[back(g)], near[g])

    for j in range(1, F):
        q_far(j).start()

    for load in loads[1:5]:
        load.wait()
    cnt = cnt_ref[...].astype(jnp.float32)
    gap = gap_ref[...].astype(jnp.float32)
    ids = pool * blocks + iota((blocks, 1), 0)
    request, usable = block_tables(bp_ref[...], cnt, gap, ids, float(tokens))
    asked = request.astype(jnp.int32)
    asked_x = lax.shift_right_logical(asked, Z.bit_length() - 1)
    slot = (
        jnp.bitwise_and(asked_x - x, X - 1) * N + jnp.bitwise_and(asked - z, N - 1)
    ) * F + lax.shift_right_logical(jnp.bitwise_and(asked, Z - 1), N.bit_length() - 1)

    own_rows = blocks * rows
    all_rows = G * frows
    slot_row = (
        jnp.broadcast_to((slot * rows)[:, None, :], (blocks, rows, 1)) + iota((blocks, rows, 1), 1)
    ).reshape(own_rows, 1)
    half = G * F * rows // X
    for j in range(X):
        pick_ref[j] = jnp.where(slot_row - j * half == iota((own_rows, half), 1), 1.0, 0.0).astype(
            jnp.bfloat16
        )

    q_own = q_ref[...].astype(jnp.float32)
    new = nk_ref[...].astype(jnp.float32)
    score0 = jnp.sum(q_own * new[0:1, :hd], axis=1, keepdims=True) * scale
    score1 = jnp.sum(q_own * new[1:2, :hd], axis=1, keepdims=True) * scale
    score1 = jnp.where(iota((rows, 1), 0) >= heads, score1, masked_value)
    new_max = jnp.maximum(score0, score1)
    weight0, weight1 = jnp.exp(score0 - new_max), jnp.exp(score1 - new_max)
    new_sum = weight0 + weight1
    new_out = (
        weight0.astype(jnp.bfloat16).astype(jnp.float32) * new[0:1, hd:]
        + weight1.astype(jnp.bfloat16).astype(jnp.float32) * new[1:2, hd:]
    ) / new_sum
    lane = iota((rows, 128), 1)
    spread = jnp.bitwise_and(lane, rows - 1) == iota((rows, 128), 0)
    new_lse = jnp.sum(
        jnp.where(spread, new_max + jnp.log(new_sum), 0.0), axis=0, keepdims=True
    )
    rl[G] = jnp.where(lax.div(iota((1, 128), 1), rows) == f, new_lse, masked_value)
    rbuf[G] = jnp.zeros((F, rows, hd), jnp.bfloat16)
    rbuf[G, f] = new_out.astype(jnp.bfloat16)

    for j in range(1, F):
        at = lax.rem(f + j, F)
        arrived(qbuf.at[0, at], rf.at[at], sf.at[0])
    for g in order:
        q_near(g).start()

    slot_lane = jnp.sum(
        jnp.where(
            lax.shift_right_logical(iota((blocks, own_rows), 1), rows.bit_length() - 1)
            == iota((blocks, own_rows), 0),
            slot, 0,
        ).astype(jnp.float32),
        axis=0, keepdims=True,
    )
    goes_to = slot_lane * rows + jnp.bitwise_and(iota((1, own_rows), 1), rows - 1).astype(
        jnp.float32
    )
    for j in range(X):
        put_ref[j] = jnp.where(
            reals((half, own_rows), 0) == goes_to - float(j * half), 1.0, 0.0
        ).astype(jnp.bfloat16)

    def dot(a, c):
        return jnp.dot(a, c, preferred_element_type=jnp.float32)

    def column(j):
        for g in (1, 3, 2) if j == 0 else (0, 1, 3, 2):
            arrived(qbuf.at[j * N + g], rp.at[j * N + g], sp.at[0])
        return dot(pick_ref[j], qbuf[j * N : (j + 1) * N].reshape(half, hd))

    nearest = sorted(range(X), key=lambda j: min(j, X - j))
    q_sel = column(0)
    for j in nearest[1:]:
        q_sel += column(j)
    q_sel = q_sel.astype(jnp.bfloat16).reshape(blocks, rows, hd)

    loads[5].wait()
    step = blocks // chunks
    position = reals((step, rows, tokens), 2)
    outs, lses = [], []
    for c in range(chunks):
        part = slice(c * step, (c + 1) * step)
        scores = jnp.einsum(
            "bqd,btd->bqt", q_sel[part], kv[part, :, :hd], preferred_element_type=jnp.float32
        ) * scale
        limit = jnp.broadcast_to(usable[part][:, None, :], (step, rows, 1))
        scores = jnp.where(position < limit, scores, masked_value)
        top = jnp.max(scores, axis=2, keepdims=True)
        weights = jnp.exp(scores - top)
        total = jnp.sum(weights, axis=2, keepdims=True)
        out = jnp.einsum(
            "bqt,btd->bqd", weights.astype(jnp.bfloat16), kv[part, :, hd:],
            preferred_element_type=jnp.float32,
        )
        outs.append(out / total)
        lses.append(jnp.sum(jnp.where(spread[None], top + jnp.log(total), 0.0), axis=1))
    out = jnp.concatenate(outs, axis=0)
    lse = jnp.concatenate(lses, axis=0)

    def o_copy(g):
        return remote(pbuf.at[g], rbuf.at[back(g)], so.at[g], ro.at[back(g)], near[g])

    def l_copy(g):
        return remote(lz.at[g], rl.at[back(g)], sl.at[g], rls.at[back(g)], near[g])

    wanted = jnp.broadcast_to(request, (blocks, 128))
    best = lse
    for k in range(blocks):
        best = jnp.maximum(
            best, jnp.where(wanted == wanted[k : k + 1], lse[k : k + 1], masked_value)
        )
    factor = jnp.exp(lse - best)
    total = jnp.zeros((blocks, 128), jnp.float32)
    for k in range(blocks):
        total += jnp.where(wanted == wanted[k : k + 1], factor[k : k + 1], 0.0)
    lse = best + jnp.log(total)
    slots = jnp.broadcast_to(slot, (blocks, 128))
    sub = lax.shift_right_logical(iota((blocks, 128), 1), rows.bit_length() - 1)
    for g in order + [0]:
        lz[g] = jnp.max(
            jnp.where(slots - g * F == sub, lse, masked_value), axis=0, keepdims=True
        )
        if g:
            l_copy(g).start()
    scaled = (out * to_column((factor / total)[:, None, :], blocks, rows)).reshape(own_rows, hd)
    high = scaled.astype(jnp.bfloat16)
    low = (scaled - high.astype(jnp.float32)).astype(jnp.bfloat16)
    both = jnp.concatenate([high, low], axis=1)
    for j in nearest[::-1]:
        put = dot(put_ref[j], both)
        pbuf[j * N : (j + 1) * N] = (
            (put[:, :hd] + put[:, hd:]).astype(jnp.bfloat16).reshape(N, F, rows, hd)
        )
        for g in order:
            if g // N == j:
                o_copy(g).start()
    rbuf[0] = pbuf[0]
    rl[0] = lz[0]

    def merged(values, count):
        high = jnp.max(values, axis=0, keepdims=True)
        factor = jnp.exp(values - high)
        total = jnp.sum(factor, axis=0, keepdims=True)
        return to_column(factor / total, count, frows), high + jnp.log(total)

    for g in order:
        arrived(rl.at[g], rls.at[g], sl.at[0])
    share, lse = merged(rl[...], G + 1)
    fl[0] = lse[0]
    acc = jnp.zeros((frows, hd), jnp.float32)
    for g in [G, 0] + order[::-1]:
        if 0 < g < G:
            arrived(rbuf.at[g], ro.at[g], so.at[0])
        acc += share[g] * rbuf[g].astype(jnp.float32).reshape(frows, hd)
    fb[0] = acc.astype(jnp.bfloat16).reshape(F, rows, hd)

    def fo_copy(j):
        return remote(fb.at[0], fb.at[F - j], sfo.at[j], rfo.at[F - j], far[j])

    def fl_copy(j):
        return remote(fl.at[0], fl.at[F - j], sfl.at[j], rfl.at[F - j], far[j])

    for j in range(1, F):
        fl_copy(j).start()
    for j in range(1, F):
        fo_copy(j).start()
    loads[6].wait()
    for j in range(1, F):
        arrived(fl.at[j], rfl.at[j], sfl.at[0])
    share, _ = merged(fl[...], F)
    acc = share[0] * fb[0].astype(jnp.float32).reshape(frows, hd)
    for j in range(1, F):
        arrived(fb.at[j], rfo.at[j], sfo.at[0])
        acc += share[j] * fb[j].astype(jnp.float32).reshape(frows, hd)
    abuf[0] = acc.astype(jnp.bfloat16).reshape(F, rows, hd)

    def a_near(g):
        return remote(abuf.at[0], abuf.at[back(g)], sg.at[g], rg.at[back(g)], near[g])

    for g in order:
        a_near(g).start()

    def y_copy(j, u, to):
        return remote(
            ysend.at[j, :, pl.ds(u * per_t, per_t)], fin.at[ten], se.at[j, u], re.at[ten],
            (pool, to),
        )

    for j in nearest:
        for g in (1, 3, 2) if j == 0 else (0, 1, 3, 2):
            arrived(abuf.at[j * N + g], rg.at[j * N + g], sg.at[0])
        for c in range(N):
            at = j * N + lax.rem(c + N - n, N)
            piece = abuf[at].astype(jnp.float32)
            for i in range(F):
                att[(i * N + c) * rows : (i * N + c + 1) * rows] = piece[i]
        halves = []
        for s in range(2):
            parts = [att[pl.ds(s * heads + h, Z, stride=rows), :] for h in range(heads)]
            halves.append(jnp.concatenate(parts, axis=1))
        a = jnp.concatenate(halves, axis=0).astype(jnp.bfloat16)
        ysend[j] = dot(a, w[...]).reshape(2, Z, w.shape[1])
        for u in range(t_per_x):
            to = xs[j] * t_per_x + u

            @pl.when(to != ten)
            def _():
                y_copy(j, u, to).start()

            @pl.when(to == ten)
            def _():
                fin[ten] = ysend[j, :, u * per_t : (u + 1) * per_t]

    for j in range(1, T):
        at = sides[j][1]
        arrived(fin.at[at], re.at[at], se.at[0, 0])
    out_ref[...] = jnp.sum(fin[...], axis=0).astype(jnp.bfloat16)

    for j in range(1, F):
        q_far(j).wait_send()
        fo_copy(j).wait_send()
        fl_copy(j).wait_send()
    for g in range(1, G):
        q_near(g).wait_send()
        l_copy(g).wait_send()
        o_copy(g).wait_send()
        a_near(g).wait_send()
    for j in range(X):
        for u in range(t_per_x):
            to = xs[j] * t_per_x + u

            @pl.when(to != ten)
            def _():
                y_copy(j, u, to).wait_send()


def body(X, Z, T, kv_pool, queries, new_kv, block_count, tail_gap, block_place, out_weight):
    blocks, _, tokens, hd2 = kv_pool.shape
    hd = hd2 // 2
    rows = 2 * queries.shape[2]
    reqs = block_count.shape[0]
    columns = out_weight.shape[1]
    F, G = Z // N, X * N
    own_rows, half = blocks * rows, N * F * rows
    dma = pltpu.SemaphoreType.DMA
    bf16, f32, i32 = jnp.bfloat16, jnp.float32, jnp.int32
    args = (
        queries.reshape(rows, hd),
        new_kv.reshape(2, hd2),
        block_count.reshape(1, reqs),
        tail_gap.reshape(1, reqs),
        block_place.reshape(1, block_place.shape[0]),
        kv_pool.reshape(blocks, tokens, hd2),
        out_weight,
    )
    return pl.pallas_call(
        functools.partial(kernel, X, Z, T),
        out_shape=jax.ShapeDtypeStruct((2, reqs // T, columns), bf16),
        in_specs=[pl.BlockSpec(memory_space=pl.ANY)] * 7,
        out_specs=pl.BlockSpec(memory_space=pltpu.VMEM),
        scratch_shapes=[pltpu.VMEM(a.shape, a.dtype) for a in args]
        + [
            pltpu.VMEM((G, F, rows, hd), bf16),
            pltpu.VMEM((X, own_rows, half), bf16),
            pltpu.VMEM((X, half, own_rows), bf16),
            pltpu.VMEM((G, F, rows, hd), bf16),
            pltpu.VMEM((G, 1, 128), f32),
            pltpu.VMEM((G + 1, F, rows, hd), bf16),
            pltpu.VMEM((G + 1, 1, 128), f32),
            pltpu.VMEM((F, F, rows, hd), bf16),
            pltpu.VMEM((F, 1, 128), f32),
            pltpu.VMEM((G, F, rows, hd), bf16),
            pltpu.VMEM((Z * rows, hd), f32),
            pltpu.VMEM((X, 2, Z, columns), f32),
            pltpu.VMEM((T, 2, reqs // T, columns), f32),
            dma((7,)),
            dma((F,)), dma((F,)),
            dma((G,)), dma((G,)),
            dma((G,)), dma((G,)), dma((G,)), dma((G,)),
            dma((F,)), dma((F,)), dma((F,)), dma((F,)),
            dma((G,)), dma((G,)),
            dma((X, Z * T // reqs)), dma((T,)),
        ],
        compiler_params=pltpu.CompilerParams(
            collective_id=0, has_side_effects=True, vmem_limit_bytes=60 * 1024 * 1024
        ),
    )(*args)


def solution(mesh):
    pools, tensors = mesh.shape["pool"], mesh.shape["tensor"]
    Z = 16 if pools == 64 else 8
    placed = (
        P("pool", "tensor", None, None),
        P(None, "pool", "tensor", None),
        P(None, "pool", "tensor", None),
        P(),
        P(),
        P(),
        P("tensor", "pool"),
    )
    return jax.shard_map(
        functools.partial(body, pools // Z, Z, tensors),
        mesh=mesh, in_specs=placed, out_specs=P(None, "tensor", "pool"), check_vma=False,
    )
```

time: 396 us -> 56.2 us (0.14)
  blocking collectives: 209 us -> 0 us
  waiting for transfers between devices: 138 us -> 0 us
  Pallas kernels: 0 us -> 54.8 us
  starting transfers between devices: 18.3 us -> 0 us
  between operations: 13.5 us -> 0.01 us
  other arithmetic: 8.01 us -> 0 us
  local copies, waits for them, and re-layouts: 5.27 us -> 1.28 us
    all_gather x3 -> x0, blocking collectives: 209 us -> none  [the longest x1 73 us: body(): lax.all_gather(queries, 'pool', axis=1, tiled=True)]
    reduce_scatter x1 -> x0, waiting for transfers between devices: 93.7 us -> none  [body(): lax.psum_scatter(partial_out, 'tensor', scatter_dimension=1, tiled=True)]
    pallas_call x0 -> x1, Pallas kernels: none -> 54.8 us  [body(): pl.pallas_call(functools.partial(kernel, X, Z, T), out_shape=jax.ShapeDty...]
    all_to_all x3 -> x0, waiting for transfers between devices: 43.9 us -> none  [the longest x1 20.5 us: body(): lax.all_to_all(req_out[None], 'pool', split_axis=2, concat_axis=0, tiled=...]
    all_to_all x3 -> x0, starting transfers between devices: 18.3 us -> none  [the longest x1 9.01 us: body(): lax.all_to_all(req_max[None], 'pool', split_axis=2, concat_axis=0, tiled=...]
  transfers between devices with their start and end apart: 4 -> 0, of which waited for: 4 -> 0; matrix products, arithmetic and copies ran while one was open for 1% -> 0% of each run, Pallas kernels for 0% -> 0%
where the time goes in v2:
time: 56.2 us; the launch traced here: 56.1 us
  Pallas kernels  54.8 us (98%)
  local copies, waits for them, and re-layouts  1.28 us (2%)
    pallas_call x1, Pallas kernels, body(): pl.pallas_call(functools.partial(kernel, X, Z, T), out_shape=jax.ShapeDty...  54.8 us
    unnamed x1, local copies, waits for them, and re-layouts  1.28 us

profile of v2, /device:TPU:1, one launch (start us, length us, event | category | flops | bytes accessed | tf_op | source)
XLA Modules:
  0.0 56.1 jit_solution(14949306436564885645)
XLA Ops:
  0.0 54.8 %shard_map.73 = bf16[2,8,128]{2,1,0:T(8,128)(2,1)} custom-call(bf16[16,128]{1,0:T(8,128)(2,1)} %bitcast.7, bf16[2,256]{1,0:T(2,128)(2,1)} %bitcast.9, s32[1,64]{1,0:T(1,128)} %bitcast.10, s32[1,64]{1,0:T(1,128)} %bitcast.11, s32[1,1024]{1,0:T(1,128)} %bitcast.8, bf16[16,256,256]{2,1,0:T(8,128)(2,1)} %bitcast.6, bf16[1024,128]{1,0:T(8,128)(2,1)} %w_hbm.1), custom_call_target="tpu_custom_call" | custom-call | tf_op jit(solution)/shard_map/pallas_call | solution.py:373
  54.8 1.3 %copy.9 = bf16[2,8,128]{2,1,0:T(8,128)(2,1)} copy(bf16[2,8,128]{2,1,0:T(8,128)(2,1)} %shard_map.73) | data formatting | bytes 8192

commit v3 on v2

--- a/solution.py
+++ b/solution.py
@@ -47,7 +47,7 @@
 def kernel(
     X, Z, T,
     q_hbm, nk_hbm, cnt_hbm, gap_hbm, bp_hbm, kv_hbm, w_hbm, out_ref,
-    q_ref, nk_ref, cnt_ref, gap_ref, bp_ref, kv, w,
+    nk_ref, cnt_ref, gap_ref, bp_ref, kv, w,
     qbuf, pick_ref, put_ref, pbuf, lz, rbuf, rl, fb, fl, abuf, att, ysend, fin,
     sem_in, sf, rf, sp, rp, so, ro, sl, rls, sfo, rfo, sfl, rfl, sg, rg, se, re,
 ):
@@ -58,7 +58,7 @@
     n, f = lax.rem(z, N), lax.div(z, N)
     blocks, tokens, hd2 = kv.shape
     hd = hd2 // 2
-    rows = q_ref.shape[0]
+    rows = q_hbm.shape[0]
     reqs = cnt_ref.shape[1]
     per_t = reqs // T
     t_per_x = Z // per_t
@@ -67,10 +67,10 @@
     frows = F * rows
 
     xs = [x] + [lax.rem(x + j, X) for j in range(1, X)]
-    hops = [0, 1, 2, Z - 1]
-    zs = [z] + [lax.rem(z + hops[j], Z) for j in range(1, N)]
+    hops = [[0, 1, 2, Z - 1], [0, 1, Z - 2, Z - 1]]
+    zs = {h: z if h == 0 else lax.rem(z + h, Z) for h in set(hops[0] + hops[1])}
     far = [(x * Z + lax.rem(z + N * j, Z), ten) for j in range(F)]
-    near = [(xs[g // N] * Z + zs[g % N], ten) for g in range(G)]
+    near = [(xs[g // N] * Z + zs[hops[g // N % 2][g % N]], ten) for g in range(G)]
     sides = [(pool, lax.rem(ten + j, T)) for j in range(T)]
 
     def back(g):
@@ -88,30 +88,37 @@
         remote(dst, dst, send, recv, far[1]).wait_recv()
 
     pairs = [
-        (q_hbm, q_ref), (bp_hbm, bp_ref), (cnt_hbm, cnt_ref), (gap_hbm, gap_ref),
+        (q_hbm, qbuf.at[0, f]), (bp_hbm, bp_ref), (cnt_hbm, cnt_ref), (gap_hbm, gap_ref),
         (nk_hbm, nk_ref), (kv_hbm, kv), (w_hbm, w),
     ]
     loads = [pltpu.make_async_copy(a, b, sem_in.at[i]) for i, (a, b) in enumerate(pairs)]
-    for load in loads:
-        load.start()
-
     barrier = pltpu.get_barrier_semaphore()
     for device in far[1:] + near[1:] + sides[1:]:
         pl.semaphore_signal(barrier, inc=1, device_id=device, device_id_type=MESH)
-    loads[0].wait()
-    qbuf[0, f] = q_ref[...]
+    for load in loads:
+        load.start()
     pl.semaphore_wait(barrier, F + G + T - 3)
 
+    def group(buf, j):
+        return buf.at[max(j * N, 1) : (j + 1) * N]
+
+    def group_arrived(buf, recv, send, j):
+        here = group(buf, j)
+        remote(here, here, send, recv.at[j], far[1]).wait_recv()
+
+    def all_sent(part, send, recv):
+        remote(part, part, send, recv, far[1]).wait_send()
+
     def q_far(j):
-        return remote(qbuf.at[0, f], qbuf.at[0, f], sf.at[j], rf.at[f], far[j])
+        return remote(q_hbm, qbuf.at[0, f], sf.at[j], rf.at[f], far[j])
 
     def q_near(g):
-        return remote(qbuf.at[0], qbuf.at[back(g)], sp.at[g], rp.at[back(g)], near[g])
+        return remote(qbuf.at[0], qbuf.at[back(g)], sp.at[0], rp.at[back(g) // N], near[g])
 
     for j in range(1, F):
         q_far(j).start()
 
-    for load in loads[1:5]:
+    for load in loads[:5]:
         load.wait()
     cnt = cnt_ref[...].astype(jnp.float32)
     gap = gap_ref[...].astype(jnp.float32)
@@ -134,7 +141,7 @@
             jnp.bfloat16
         )
 
-    q_own = q_ref[...].astype(jnp.float32)
+    q_own = qbuf[0, f].astype(jnp.float32)
     new = nk_ref[...].astype(jnp.float32)
     score0 = jnp.sum(q_own * new[0:1, :hd], axis=1, keepdims=True) * scale
     score1 = jnp.sum(q_own * new[1:2, :hd], axis=1, keepdims=True) * scale
@@ -181,8 +188,7 @@
         return jnp.dot(a, c, preferred_element_type=jnp.float32)
 
     def column(j):
-        for g in (1, 3, 2) if j == 0 else (0, 1, 3, 2):
-            arrived(qbuf.at[j * N + g], rp.at[j * N + g], sp.at[0])
+        group_arrived(qbuf, rp, sp.at[0], j)
         return dot(pick_ref[j], qbuf[j * N : (j + 1) * N].reshape(half, hd))
 
     nearest = sorted(range(X), key=lambda j: min(j, X - j))
@@ -215,10 +221,10 @@
     lse = jnp.concatenate(lses, axis=0)
 
     def o_copy(g):
-        return remote(pbuf.at[g], rbuf.at[back(g)], so.at[g], ro.at[back(g)], near[g])
+        return remote(pbuf.at[g], rbuf.at[back(g)], so.at[0], ro.at[back(g) // N], near[g])
 
     def l_copy(g):
-        return remote(lz.at[g], rl.at[back(g)], sl.at[g], rls.at[back(g)], near[g])
+        return remote(lz.at[g], rl.at[back(g)], sl.at[0], rls.at[0], near[g])
 
     wanted = jnp.broadcast_to(request, (blocks, 128))
     best = lse
@@ -260,15 +266,15 @@
         total = jnp.sum(factor, axis=0, keepdims=True)
         return to_column(factor / total, count, frows), high + jnp.log(total)
 
-    for g in order:
-        arrived(rl.at[g], rls.at[g], sl.at[0])
+    arrived(rl.at[1:G], rls.at[0], sl.at[0])
     share, lse = merged(rl[...], G + 1)
     fl[0] = lse[0]
     acc = jnp.zeros((frows, hd), jnp.float32)
-    for g in [G, 0] + order[::-1]:
-        if 0 < g < G:
-            arrived(rbuf.at[g], ro.at[g], so.at[0])
-        acc += share[g] * rbuf[g].astype(jnp.float32).reshape(frows, hd)
+    acc += share[G] * rbuf[G].astype(jnp.float32).reshape(frows, hd)
+    for j in nearest:
+        group_arrived(rbuf, ro, so.at[0], j)
+        for g in range(j * N, (j + 1) * N):
+            acc += share[g] * rbuf[g].astype(jnp.float32).reshape(frows, hd)
     fb[0] = acc.astype(jnp.bfloat16).reshape(F, rows, hd)
 
     def fo_copy(j):
@@ -292,20 +298,27 @@
     abuf[0] = acc.astype(jnp.bfloat16).reshape(F, rows, hd)
 
     def a_near(g):
-        return remote(abuf.at[0], abuf.at[back(g)], sg.at[g], rg.at[back(g)], near[g])
+        return remote(abuf.at[0], abuf.at[back(g)], sg.at[0], rg.at[back(g) // N], near[g])
 
     for g in order:
         a_near(g).start()
 
+    for j in range(1, F):
+        q_far(j).wait_send()
+        fo_copy(j).wait_send()
+        fl_copy(j).wait_send()
+    all_sent(qbuf.at[1:G], sp.at[0], rp.at[0])
+    all_sent(lz.at[1:G], sl.at[0], rls.at[0])
+    all_sent(pbuf.at[1:G], so.at[0], ro.at[0])
+
     def y_copy(j, u, to):
         return remote(
-            ysend.at[j, :, pl.ds(u * per_t, per_t)], fin.at[ten], se.at[j, u], re.at[ten],
-            (pool, to),
+            ysend.at[j, :, pl.ds(u * per_t, per_t)], fin.at[lax.rem(ten + T - to, T)],
+            se.at[0], re.at[0], (pool, to),
         )
 
     for j in nearest:
-        for g in (1, 3, 2) if j == 0 else (0, 1, 3, 2):
-            arrived(abuf.at[j * N + g], rg.at[j * N + g], sg.at[0])
+        group_arrived(abuf, rg, sg.at[0], j)
         for c in range(N):
             at = j * N + lax.rem(c + N - n, N)
             piece = abuf[at].astype(jnp.float32)
@@ -326,29 +339,12 @@
 
             @pl.when(to == ten)
             def _():
-                fin[ten] = ysend[j, :, u * per_t : (u + 1) * per_t]
-
-    for j in range(1, T):
-        at = sides[j][1]
-        arrived(fin.at[at], re.at[at], se.at[0, 0])
+                fin[0] = ysend[j, :, u * per_t : (u + 1) * per_t]
+
+    all_sent(abuf.at[1:G], sg.at[0], rg.at[0])
+    arrived(fin.at[1:T], re.at[0], se.at[0])
     out_ref[...] = jnp.sum(fin[...], axis=0).astype(jnp.bfloat16)
-
-    for j in range(1, F):
-        q_far(j).wait_send()
-        fo_copy(j).wait_send()
-        fl_copy(j).wait_send()
-    for g in range(1, G):
-        q_near(g).wait_send()
-        l_copy(g).wait_send()
-        o_copy(g).wait_send()
-        a_near(g).wait_send()
-    for j in range(X):
-        for u in range(t_per_x):
-            to = xs[j] * t_per_x + u
-
-            @pl.when(to != ten)
-            def _():
-                y_copy(j, u, to).wait_send()
+    all_sent(fin.at[1:T], se.at[0], re.at[0])
 
 
 def body(X, Z, T, kv_pool, queries, new_kv, block_count, tail_gap, block_place, out_weight):
@@ -375,7 +371,7 @@
         out_shape=jax.ShapeDtypeStruct((2, reqs // T, columns), bf16),
         in_specs=[pl.BlockSpec(memory_space=pl.ANY)] * 7,
         out_specs=pl.BlockSpec(memory_space=pltpu.VMEM),
-        scratch_shapes=[pltpu.VMEM(a.shape, a.dtype) for a in args]
+        scratch_shapes=[pltpu.VMEM(a.shape, a.dtype) for a in args[1:]]
         + [
             pltpu.VMEM((G, F, rows, hd), bf16),
             pltpu.VMEM((X, own_rows, half), bf16),
@@ -392,11 +388,11 @@
             pltpu.VMEM((T, 2, reqs // T, columns), f32),
             dma((7,)),
             dma((F,)), dma((F,)),
-            dma((G,)), dma((G,)),
-            dma((G,)), dma((G,)), dma((G,)), dma((G,)),
+            dma((1,)), dma((X,)),
+            dma((1,)), dma((X,)), dma((1,)), dma((1,)),
             dma((F,)), dma((F,)), dma((F,)), dma((F,)),
-            dma((G,)), dma((G,)),
-            dma((X, Z * T // reqs)), dma((T,)),
+            dma((1,)), dma((X,)),
+            dma((1,)), dma((1,)),
         ],
         compiler_params=pltpu.CompilerParams(
             collective_id=0, has_side_effects=True, vmem_limit_bytes=60 * 1024 * 1024

time: 56.2 us -> 55.2 us (0.982)
  Pallas kernels: 54.8 us -> 53.8 us
    pallas_call x1, Pallas kernels: 54.8 us -> 53.8 us  [body(): pl.pallas_call(functools.partial(kernel, X, Z, T), out_shape=jax.ShapeDty...]
where the time goes in v3:
time: 55.2 us; the launch traced here: 55.1 us
  Pallas kernels  53.8 us (97%)
  local copies, waits for them, and re-layouts  1.28 us (2%)
    pallas_call x1, Pallas kernels, body(): pl.pallas_call(functools.partial(kernel, X, Z, T), out_shape=jax.ShapeDty...  53.8 us
    unnamed x1, local copies, waits for them, and re-layouts  1.28 us

profile of v3, /device:TPU:1, one launch (start us, length us, event | category | flops | bytes accessed | tf_op | source)
XLA Modules:
  0.0 55.1 jit_solution(17170914975632903611)
XLA Ops:
  0.0 53.8 %shard_map.73 = bf16[2,8,128]{2,1,0:T(8,128)(2,1)} custom-call(bf16[16,128]{1,0:T(8,128)(2,1)} %bitcast.7, bf16[2,256]{1,0:T(2,128)(2,1)} %bitcast.9, s32[1,64]{1,0:T(1,128)} %bitcast.10, s32[1,64]{1,0:T(1,128)} %bitcast.11, s32[1,1024]{1,0:T(1,128)} %bitcast.8, bf16[16,256,256]{2,1,0:T(8,128)(2,1)} %bitcast.6, bf16[1024,128]{1,0:T(8,128)(2,1)} %w_hbm.1), custom_call_target="tpu_custom_call" | custom-call | tf_op jit(solution)/shard_map/pallas_call | solution.py:369
  53.8 1.3 %copy.9 = bf16[2,8,128]{2,1,0:T(8,128)(2,1)} copy(bf16[2,8,128]{2,1,0:T(8,128)(2,1)} %shard_map.73) | data formatting | bytes 8192

commit v4 on v3

--- a/solution.py
+++ b/solution.py
@@ -10,7 +10,7 @@
 MESH = pl.DeviceIdType.MESH
 masked_value = -1e30
 N = 4
-chunks = 4
+chunks = 2
 
 
 def iota(shape, axis):
@@ -48,7 +48,7 @@
     X, Z, T,
     q_hbm, nk_hbm, cnt_hbm, gap_hbm, bp_hbm, kv_hbm, w_hbm, out_ref,
     nk_ref, cnt_ref, gap_ref, bp_ref, kv, w,
-    qbuf, pick_ref, put_ref, pbuf, lz, rbuf, rl, fb, fl, abuf, att, ysend, fin,
+    qbuf, pick_ref, put_ref, slot_ref, goes_ref, limit_ref, qsel_ref, out_blocks, lse_ref, pbuf, lz, rbuf, rl, fb, fl, abuf, att, ysend, fin,
     sem_in, sf, rf, sp, rp, so, ro, sl, rls, sfo, rfo, sfl, rfl, sg, rg, se, re,
 ):
     pool, ten = lax.axis_index("pool"), lax.axis_index("tensor")
@@ -61,7 +61,6 @@
     rows = q_hbm.shape[0]
     reqs = cnt_ref.shape[1]
     per_t = reqs // T
-    t_per_x = Z // per_t
     heads = rows // 2
     scale = hd ** (-0.5)
     frows = F * rows
@@ -92,15 +91,34 @@
         (nk_hbm, nk_ref), (kv_hbm, kv), (w_hbm, w),
     ]
     loads = [pltpu.make_async_copy(a, b, sem_in.at[i]) for i, (a, b) in enumerate(pairs)]
+    loads[0].start()
     barrier = pltpu.get_barrier_semaphore()
     for device in far[1:] + near[1:] + sides[1:]:
         pl.semaphore_signal(barrier, inc=1, device_id=device, device_id_type=MESH)
-    for load in loads:
+    for load in loads[1:]:
         load.start()
+    loads[0].wait()
     pl.semaphore_wait(barrier, F + G + T - 3)
 
     def group(buf, j):
-        return buf.at[max(j * N, 1) : (j + 1) * N]
+        if isinstance(j, int):
+            return buf.at[max(j * N, 1) : (j + 1) * N]
+        return buf.at[pl.ds(j * N, N)]
+
+    fh = F // 2
+    parts_f = [pl.ds(0, fh), pl.ds(fh, fh)]
+    hrows = fh * rows
+
+    def half_arrived(buf, recv, send, j, p):
+        here = group(buf, j).at[:, parts_f[p]]
+        remote(here, here, send, recv.at[p * X + j], near[1]).wait_recv()
+
+    def loop(low, high, body):
+        def once(i, carry):
+            body(i)
+            return carry
+
+        lax.fori_loop(low, high, once, 0)
 
     def group_arrived(buf, recv, send, j):
         here = group(buf, j)
@@ -110,7 +128,7 @@
         remote(part, part, send, recv, far[1]).wait_send()
 
     def q_far(j):
-        return remote(q_hbm, qbuf.at[0, f], sf.at[j], rf.at[f], far[j])
+        return remote(qbuf.at[0, f], qbuf.at[0, f], sf.at[j], rf.at[f], far[j])
 
     def q_near(g):
         return remote(qbuf.at[0], qbuf.at[back(g)], sp.at[0], rp.at[back(g) // N], near[g])
@@ -118,7 +136,7 @@
     for j in range(1, F):
         q_far(j).start()
 
-    for load in loads[:5]:
+    for load in loads[1:5]:
         load.wait()
     cnt = cnt_ref[...].astype(jnp.float32)
     gap = gap_ref[...].astype(jnp.float32)
@@ -130,16 +148,22 @@
         jnp.bitwise_and(asked_x - x, X - 1) * N + jnp.bitwise_and(asked - z, N - 1)
     ) * F + lax.shift_right_logical(jnp.bitwise_and(asked, Z - 1), N.bit_length() - 1)
 
+    for b in range(blocks):
+        limit_ref[b] = jnp.broadcast_to(usable[b : b + 1], (1, 128))
+
     own_rows = blocks * rows
     all_rows = G * frows
     slot_row = (
         jnp.broadcast_to((slot * rows)[:, None, :], (blocks, rows, 1)) + iota((blocks, rows, 1), 1)
     ).reshape(own_rows, 1)
     half = G * F * rows // X
-    for j in range(X):
-        pick_ref[j] = jnp.where(slot_row - j * half == iota((own_rows, half), 1), 1.0, 0.0).astype(
-            jnp.bfloat16
-        )
+    slot_ref[...] = jnp.broadcast_to(slot_row, (own_rows, 128))
+
+    def fill_pick(j):
+        here = slot_ref[...][:, :1] - j * half == iota((own_rows, half), 1)
+        pick_ref[j] = jnp.where(here, 1.0, 0.0).astype(jnp.bfloat16)
+
+    loop(0, X, fill_pick)
 
     q_own = qbuf[0, f].astype(jnp.float32)
     new = nk_ref[...].astype(jnp.float32)
@@ -179,10 +203,17 @@
     goes_to = slot_lane * rows + jnp.bitwise_and(iota((1, own_rows), 1), rows - 1).astype(
         jnp.float32
     )
-    for j in range(X):
-        put_ref[j] = jnp.where(
-            reals((half, own_rows), 0) == goes_to - float(j * half), 1.0, 0.0
-        ).astype(jnp.bfloat16)
+    goes_ref[...] = goes_to
+
+    row = iota((N * hrows, own_rows), 0)
+    row = (row + lax.shift_right_logical(row, hrows.bit_length() - 1) * hrows).astype(jnp.float32)
+
+    def fill_put(i):
+        first = lax.rem(i, X) * half + lax.div(i, X) * hrows
+        here = goes_ref[...] - first.astype(jnp.float32) == row
+        put_ref[i] = jnp.where(here, 1.0, 0.0).astype(jnp.bfloat16)
+
+    loop(0, 2 * X, fill_put)
 
     def dot(a, c):
         return jnp.dot(a, c, preferred_element_type=jnp.float32)
@@ -195,18 +226,19 @@
     q_sel = column(0)
     for j in nearest[1:]:
         q_sel += column(j)
-    q_sel = q_sel.astype(jnp.bfloat16).reshape(blocks, rows, hd)
+    qsel_ref[...] = q_sel.astype(jnp.bfloat16).reshape(blocks, rows, hd)
 
     loads[5].wait()
     step = blocks // chunks
     position = reals((step, rows, tokens), 2)
-    outs, lses = [], []
-    for c in range(chunks):
-        part = slice(c * step, (c + 1) * step)
+
+    def attend(c):
+        part = pl.ds(c * step, step)
         scores = jnp.einsum(
-            "bqd,btd->bqt", q_sel[part], kv[part, :, :hd], preferred_element_type=jnp.float32
+            "bqd,btd->bqt", qsel_ref[part], kv[part, :, :hd], preferred_element_type=jnp.float32
         ) * scale
-        limit = jnp.broadcast_to(usable[part][:, None, :], (step, rows, 1))
+        limit = jnp.broadcast_to(limit_ref[part], (step, 1, 128))
+        limit = jnp.concatenate([limit] * (tokens // 128), axis=2)
         scores = jnp.where(position < limit, scores, masked_value)
         top = jnp.max(scores, axis=2, keepdims=True)
         weights = jnp.exp(scores - top)
@@ -215,13 +247,18 @@
             "bqt,btd->bqd", weights.astype(jnp.bfloat16), kv[part, :, hd:],
             preferred_element_type=jnp.float32,
         )
-        outs.append(out / total)
-        lses.append(jnp.sum(jnp.where(spread[None], top + jnp.log(total), 0.0), axis=1))
-    out = jnp.concatenate(outs, axis=0)
-    lse = jnp.concatenate(lses, axis=0)
-
-    def o_copy(g):
-        return remote(pbuf.at[g], rbuf.at[back(g)], so.at[0], ro.at[back(g) // N], near[g])
+        out_blocks[part] = out / total
+        lse_ref[c] = jnp.sum(jnp.where(spread[None], top + jnp.log(total), 0.0), axis=1)
+
+    loop(0, chunks, attend)
+    out = out_blocks[...]
+    lse = lse_ref[...].reshape(blocks, 128)
+
+    def o_copy(g, p):
+        part = parts_f[p]
+        return remote(
+            pbuf.at[g, part], rbuf.at[back(g), part], so.at[0], ro.at[p * X + back(g) // N], near[g]
+        )
 
     def l_copy(g):
         return remote(lz.at[g], rl.at[back(g)], sl.at[0], rls.at[0], near[g])
@@ -239,24 +276,24 @@
     lse = best + jnp.log(total)
     slots = jnp.broadcast_to(slot, (blocks, 128))
     sub = lax.shift_right_logical(iota((blocks, 128), 1), rows.bit_length() - 1)
-    for g in order + [0]:
-        lz[g] = jnp.max(
-            jnp.where(slots - g * F == sub, lse, masked_value), axis=0, keepdims=True
-        )
-        if g:
-            l_copy(g).start()
     scaled = (out * to_column((factor / total)[:, None, :], blocks, rows)).reshape(own_rows, hd)
     high = scaled.astype(jnp.bfloat16)
     low = (scaled - high.astype(jnp.float32)).astype(jnp.bfloat16)
     both = jnp.concatenate([high, low], axis=1)
-    for j in nearest[::-1]:
-        put = dot(put_ref[j], both)
-        pbuf[j * N : (j + 1) * N] = (
-            (put[:, :hd] + put[:, hd:]).astype(jnp.bfloat16).reshape(N, F, rows, hd)
-        )
+    for i, (p, j) in enumerate([(p, j) for p in range(2) for j in nearest[::-1]]):
+        put = dot(put_ref[p * X + j], both)
+        put = (put[:, :hd] + put[:, hd:]).astype(jnp.bfloat16)
+        pbuf[j * N : (j + 1) * N, p * fh : (p + 1) * fh] = put.reshape(N, fh, rows, hd)
         for g in order:
             if g // N == j:
-                o_copy(g).start()
+                o_copy(g, p).start()
+        if i == 0:
+            for g in order + [0]:
+                lz[g] = jnp.max(
+                    jnp.where(slots - g * F == sub, lse, masked_value), axis=0, keepdims=True
+                )
+                if g:
+                    l_copy(g).start()
     rbuf[0] = pbuf[0]
     rl[0] = lz[0]
 
@@ -269,78 +306,95 @@
     arrived(rl.at[1:G], rls.at[0], sl.at[0])
     share, lse = merged(rl[...], G + 1)
     fl[0] = lse[0]
-    acc = jnp.zeros((frows, hd), jnp.float32)
-    acc += share[G] * rbuf[G].astype(jnp.float32).reshape(frows, hd)
-    for j in nearest:
-        group_arrived(rbuf, ro, so.at[0], j)
-        for g in range(j * N, (j + 1) * N):
-            acc += share[g] * rbuf[g].astype(jnp.float32).reshape(frows, hd)
-    fb[0] = acc.astype(jnp.bfloat16).reshape(F, rows, hd)
-
-    def fo_copy(j):
-        return remote(fb.at[0], fb.at[F - j], sfo.at[j], rfo.at[F - j], far[j])
+
+    def fo_copy(j, p):
+        part = parts_f[p]
+        return remote(
+            fb.at[0, part], fb.at[F - j, part], sfo.at[p * F + j], rfo.at[p * F + F - j], far[j]
+        )
 
     def fl_copy(j):
         return remote(fl.at[0], fl.at[F - j], sfl.at[j], rfl.at[F - j], far[j])
 
+    def weighted(share, buf, g, p):
+        here = buf[g, p * fh : (p + 1) * fh].astype(jnp.float32).reshape(hrows, hd)
+        return share[g][p * hrows : (p + 1) * hrows] * here
+
+    def stored(acc):
+        return acc.astype(jnp.bfloat16).reshape(fh, rows, hd)
+
     for j in range(1, F):
         fl_copy(j).start()
-    for j in range(1, F):
-        fo_copy(j).start()
+    for p in range(2):
+        acc = weighted(share, rbuf, G, p)
+        for j in nearest:
+            half_arrived(rbuf, ro, so.at[0], j, p)
+            for g in range(j * N, (j + 1) * N):
+                acc += weighted(share, rbuf, g, p)
+        fb[0, p * fh : (p + 1) * fh] = stored(acc)
+        for j in range(1, F):
+            fo_copy(j, p).start()
     loads[6].wait()
     for j in range(1, F):
         arrived(fl.at[j], rfl.at[j], sfl.at[0])
     share, _ = merged(fl[...], F)
-    acc = share[0] * fb[0].astype(jnp.float32).reshape(frows, hd)
-    for j in range(1, F):
-        arrived(fb.at[j], rfo.at[j], sfo.at[0])
-        acc += share[j] * fb[j].astype(jnp.float32).reshape(frows, hd)
-    abuf[0] = acc.astype(jnp.bfloat16).reshape(F, rows, hd)
-
-    def a_near(g):
-        return remote(abuf.at[0], abuf.at[back(g)], sg.at[0], rg.at[back(g) // N], near[g])
-
-    for g in order:
-        a_near(g).start()
+
+    def a_near(g, p):
+        part = parts_f[p]
+        return remote(
+            abuf.at[0, part], abuf.at[back(g), part], sg.at[0], rg.at[p * X + back(g) // N], near[g]
+        )
+
+    for p in range(2):
+        acc = weighted(share, fb, 0, p)
+        for j in range(1, F):
+            here = fb.at[j, parts_f[p]]
+            arrived(here, rfo.at[p * F + j], sfo.at[0])
+            acc += weighted(share, fb, j, p)
+        abuf[0, p * fh : (p + 1) * fh] = stored(acc)
+        for g in order:
+            a_near(g, p).start()
 
     for j in range(1, F):
         q_far(j).wait_send()
-        fo_copy(j).wait_send()
+        fo_copy(j, 0).wait_send()
+        fo_copy(j, 1).wait_send()
         fl_copy(j).wait_send()
     all_sent(qbuf.at[1:G], sp.at[0], rp.at[0])
     all_sent(lz.at[1:G], sl.at[0], rls.at[0])
     all_sent(pbuf.at[1:G], so.at[0], ro.at[0])
 
-    def y_copy(j, u, to):
+    def y_copy(j, p, to):
         return remote(
-            ysend.at[j, :, pl.ds(u * per_t, per_t)], fin.at[lax.rem(ten + T - to, T)],
-            se.at[0], re.at[0], (pool, to),
-        )
-
-    for j in nearest:
-        group_arrived(abuf, rg, sg.at[0], j)
+            ysend.at[p, j], fin.at[lax.rem(ten + T - to, T)], se.at[0], re.at[0], (pool, to)
+        )
+
+    def project(j, p):
+        half_arrived(abuf, rg, sg.at[0], j, p)
         for c in range(N):
             at = j * N + lax.rem(c + N - n, N)
-            piece = abuf[at].astype(jnp.float32)
-            for i in range(F):
+            piece = abuf[at, p * fh : (p + 1) * fh].astype(jnp.float32)
+            for i in range(fh):
                 att[(i * N + c) * rows : (i * N + c + 1) * rows] = piece[i]
         halves = []
         for s in range(2):
-            parts = [att[pl.ds(s * heads + h, Z, stride=rows), :] for h in range(heads)]
+            parts = [att[pl.ds(s * heads + h, per_t, stride=rows), :] for h in range(heads)]
             halves.append(jnp.concatenate(parts, axis=1))
         a = jnp.concatenate(halves, axis=0).astype(jnp.bfloat16)
-        ysend[j] = dot(a, w[...]).reshape(2, Z, w.shape[1])
-        for u in range(t_per_x):
-            to = xs[j] * t_per_x + u
-
-            @pl.when(to != ten)
-            def _():
-                y_copy(j, u, to).start()
-
-            @pl.when(to == ten)
-            def _():
-                fin[0] = ysend[j, :, u * per_t : (u + 1) * per_t]
-
+        ysend[p, j] = dot(a, w[...]).reshape(2, per_t, w.shape[1])
+        to = lax.rem(x + j, X) * 2 + p
+
+        @pl.when(to != ten)
+        def _():
+            y_copy(j, p, to).start()
+
+        @pl.when(to == ten)
+        def _():
+            fin[0] = ysend[p, j]
+
+    for p in range(2):
+        project(0, p)
+        loop(1, X, lambda i: project(i + lax.div(i, 2) * (1 - 2 * lax.rem(i, 2)), p))
     all_sent(abuf.at[1:G], sg.at[0], rg.at[0])
     arrived(fin.at[1:T], re.at[0], se.at[0])
     out_ref[...] = jnp.sum(fin[...], axis=0).astype(jnp.bfloat16)
@@ -375,7 +429,13 @@
         + [
             pltpu.VMEM((G, F, rows, hd), bf16),
             pltpu.VMEM((X, own_rows, half), bf16),
-            pltpu.VMEM((X, half, own_rows), bf16),
+            pltpu.VMEM((2 * X, half // 2, own_rows), bf16),
+            pltpu.VMEM((own_rows, 128), i32),
+            pltpu.VMEM((1, own_rows), f32),
+            pltpu.VMEM((blocks, 1, 128), f32),
+            pltpu.VMEM((blocks, rows, hd), bf16),
+            pltpu.VMEM((blocks, rows, hd), f32),
+            pltpu.VMEM((chunks, blocks // chunks, 128), f32),
             pltpu.VMEM((G, F, rows, hd), bf16),
             pltpu.VMEM((G, 1, 128), f32),
             pltpu.VMEM((G + 1, F, rows, hd), bf16),
@@ -383,26 +443,26 @@
             pltpu.VMEM((F, F, rows, hd), bf16),
             pltpu.VMEM((F, 1, 128), f32),
             pltpu.VMEM((G, F, rows, hd), bf16),
-            pltpu.VMEM((Z * rows, hd), f32),
-            pltpu.VMEM((X, 2, Z, columns), f32),
+            pltpu.VMEM((Z * rows // 2, hd), f32),
+            pltpu.VMEM((2, X, 2, reqs // T, columns), f32),
             pltpu.VMEM((T, 2, reqs // T, columns), f32),
             dma((7,)),
             dma((F,)), dma((F,)),
             dma((1,)), dma((X,)),
-            dma((1,)), dma((X,)), dma((1,)), dma((1,)),
-            dma((F,)), dma((F,)), dma((F,)), dma((F,)),
-            dma((1,)), dma((X,)),
+            dma((1,)), dma((2 * X,)), dma((1,)), dma((1,)),
+            dma((2 * F,)), dma((2 * F,)), dma((F,)), dma((F,)),
+            dma((1,)), dma((2 * X,)),
             dma((1,)), dma((1,)),
         ],
         compiler_params=pltpu.CompilerParams(
-            collective_id=0, has_side_effects=True, vmem_limit_bytes=60 * 1024 * 1024
+            collective_id=0, has_side_effects=True, vmem_limit_bytes=40 * 1024 * 1024
         ),
-    )(*args)
+    )(*[pltpu.with_memory_space_constraint(a, pltpu.HBM) for a in args])
 
 
 def solution(mesh):
     pools, tensors = mesh.shape["pool"], mesh.shape["tensor"]
-    Z = 16 if pools == 64 else 8
+    Z = 16
     placed = (
         P("pool", "tensor", None, None),
         P(None, "pool", "tensor", None),

time: 55.2 us -> 54 us (0.978)
  local copies, waits for them, and re-layouts: 1.28 us -> 0.6 us
  Pallas kernels: 53.8 us -> 53.2 us
    unnamed x1, local copies, waits for them, and re-layouts: 1.28 us -> 0.6 us
    pallas_call x1, Pallas kernels: 53.8 us -> 53.2 us  [body(): pl.pallas_call(functools.partial(kernel, X, Z, T), out_shape=jax.ShapeDty...]
where the time goes in v4:
time: 54 us; the launch traced here: 53.8 us
  Pallas kernels  53.2 us (99%)
  local copies, waits for them, and re-layouts  0.6 us (1%)
    pallas_call x1, Pallas kernels, body(): pl.pallas_call(functools.partial(kernel, X, Z, T), out_shape=jax.ShapeDty...  53.2 us

profile of v4, /device:TPU:1, one launch (start us, length us, event | category | flops | bytes accessed | tf_op | source)
XLA Modules:
  0.0 53.8 jit_solution(8325367191321580472)
XLA Ops:
  0.0 53.2 %shard_map.73 = bf16[2,8,128]{2,1,0:T(8,128)(2,1)S(1)} custom-call(bf16[16,128]{1,0:T(8,128)(2,1)} %bitcast.7, bf16[2,256]{1,0:T(2,128)(2,1)} %bitcast.9, s32[1,64]{1,0:T(1,128)} %bitcast.10, s32[1,64]{1,0:T(1,128)} %bitcast.11, s32[1,1024]{1,0:T(1,128)} %bitcast.8, bf16[16,256,256]{2,1,0:T(8,128)(2,1)} %bitcast.6, bf16[1024,128]{1,0:T(8,128)(2,1)} %w_hbm.1), custom_call_target="tpu_custom_call" | custom-call | tf_op jit(solution)/shard_map/pallas_call | solution.py:423
  53.3 0.6 %copy.9 = bf16[2,8,128]{2,1,0:T(8,128)(2,1)} copy(bf16[2,8,128]{2,1,0:T(8,128)(2,1)S(1)} %shard_map.73) | data formatting | bytes 8192

commit v5 on v3

--- a/solution.py
+++ b/solution.py
@@ -10,7 +10,7 @@
 MESH = pl.DeviceIdType.MESH
 masked_value = -1e30
 N = 4
-chunks = 4
+chunks = 2
 
 
 def iota(shape, axis):
@@ -44,12 +44,21 @@
     )
 
 
+def in_three(values, rows):
+    high = values.astype(jnp.bfloat16).astype(jnp.float32)
+    middle = (values - high).astype(jnp.bfloat16).astype(jnp.float32)
+    low = values - high - middle
+    row = iota((rows, 128), 0)
+    tile = jnp.where(row == 0, high, jnp.where(row == 1, middle, jnp.where(row == 2, low, 0.0)))
+    return tile.astype(jnp.bfloat16)
+
+
 def kernel(
     X, Z, T,
     q_hbm, nk_hbm, cnt_hbm, gap_hbm, bp_hbm, kv_hbm, w_hbm, out_ref,
     nk_ref, cnt_ref, gap_ref, bp_ref, kv, w,
-    qbuf, pick_ref, put_ref, pbuf, lz, rbuf, rl, fb, fl, abuf, att, ysend, fin,
-    sem_in, sf, rf, sp, rp, so, ro, sl, rls, sfo, rfo, sfl, rfl, sg, rg, se, re,
+    qbuf, pick_ref, put_ref, slot_ref, goes_ref, limit_ref, qsel_ref, out_blocks, lse_ref, pbuf, rbuf, fb, abuf, att, ysend, fin,
+    sem_in, sf, rf, sp, rp, so, ro, sfo, rfo, sg, rg, se, re,
 ):
     pool, ten = lax.axis_index("pool"), lax.axis_index("tensor")
     x, z = lax.div(pool, Z), lax.rem(pool, Z)
@@ -92,15 +101,26 @@
         (nk_hbm, nk_ref), (kv_hbm, kv), (w_hbm, w),
     ]
     loads = [pltpu.make_async_copy(a, b, sem_in.at[i]) for i, (a, b) in enumerate(pairs)]
+    loads[0].start()
     barrier = pltpu.get_barrier_semaphore()
     for device in far[1:] + near[1:] + sides[1:]:
         pl.semaphore_signal(barrier, inc=1, device_id=device, device_id_type=MESH)
-    for load in loads:
+    for load in loads[1:]:
         load.start()
+    loads[0].wait()
     pl.semaphore_wait(barrier, F + G + T - 3)
 
     def group(buf, j):
-        return buf.at[max(j * N, 1) : (j + 1) * N]
+        if isinstance(j, int):
+            return buf.at[max(j * N, 1) : (j + 1) * N]
+        return buf.at[pl.ds(j * N, N)]
+
+    def loop(low, high, body):
+        def once(i, carry):
+            body(i)
+            return carry
+
+        lax.fori_loop(low, high, once, 0)
 
     def group_arrived(buf, recv, send, j):
         here = group(buf, j)
@@ -110,7 +130,7 @@
         remote(part, part, send, recv, far[1]).wait_send()
 
     def q_far(j):
-        return remote(q_hbm, qbuf.at[0, f], sf.at[j], rf.at[f], far[j])
+        return remote(qbuf.at[0, f], qbuf.at[0, f], sf.at[j], rf.at[f], far[j])
 
     def q_near(g):
         return remote(qbuf.at[0], qbuf.at[back(g)], sp.at[0], rp.at[back(g) // N], near[g])
@@ -118,7 +138,7 @@
     for j in range(1, F):
         q_far(j).start()
 
-    for load in loads[:5]:
+    for load in loads[1:5]:
         load.wait()
     cnt = cnt_ref[...].astype(jnp.float32)
     gap = gap_ref[...].astype(jnp.float32)
@@ -130,16 +150,22 @@
         jnp.bitwise_and(asked_x - x, X - 1) * N + jnp.bitwise_and(asked - z, N - 1)
     ) * F + lax.shift_right_logical(jnp.bitwise_and(asked, Z - 1), N.bit_length() - 1)
 
+    for b in range(blocks):
+        limit_ref[b] = jnp.broadcast_to(usable[b : b + 1], (1, 128))
+
     own_rows = blocks * rows
     all_rows = G * frows
     slot_row = (
         jnp.broadcast_to((slot * rows)[:, None, :], (blocks, rows, 1)) + iota((blocks, rows, 1), 1)
     ).reshape(own_rows, 1)
     half = G * F * rows // X
-    for j in range(X):
-        pick_ref[j] = jnp.where(slot_row - j * half == iota((own_rows, half), 1), 1.0, 0.0).astype(
-            jnp.bfloat16
-        )
+    slot_ref[...] = jnp.broadcast_to(slot_row, (own_rows, 128))
+
+    def fill_pick(j):
+        here = slot_ref[...][:, :1] - j * half == iota((own_rows, half), 1)
+        pick_ref[j] = jnp.where(here, 1.0, 0.0).astype(jnp.bfloat16)
+
+    loop(0, X, fill_pick)
 
     q_own = qbuf[0, f].astype(jnp.float32)
     new = nk_ref[...].astype(jnp.float32)
@@ -158,8 +184,9 @@
     new_lse = jnp.sum(
         jnp.where(spread, new_max + jnp.log(new_sum), 0.0), axis=0, keepdims=True
     )
-    rl[G] = jnp.where(lax.div(iota((1, 128), 1), rows) == f, new_lse, masked_value)
-    rbuf[G] = jnp.zeros((F, rows, hd), jnp.bfloat16)
+    rbuf[G] = jnp.zeros((F + 1, rows, hd), jnp.bfloat16)
+    new_lse = jnp.where(lax.div(iota((1, 128), 1), rows) == f, new_lse, masked_value)
+    rbuf[G, F] = in_three(new_lse, rows)
     rbuf[G, f] = new_out.astype(jnp.bfloat16)
 
     for j in range(1, F):
@@ -179,10 +206,13 @@
     goes_to = slot_lane * rows + jnp.bitwise_and(iota((1, own_rows), 1), rows - 1).astype(
         jnp.float32
     )
-    for j in range(X):
-        put_ref[j] = jnp.where(
-            reals((half, own_rows), 0) == goes_to - float(j * half), 1.0, 0.0
-        ).astype(jnp.bfloat16)
+    goes_ref[...] = goes_to
+
+    def fill_put(j):
+        here = goes_ref[...] - (j * half).astype(jnp.float32) == reals((half, own_rows), 0)
+        put_ref[j] = jnp.where(here, 1.0, 0.0).astype(jnp.bfloat16)
+
+    loop(0, X, fill_put)
 
     def dot(a, c):
         return jnp.dot(a, c, preferred_element_type=jnp.float32)
@@ -195,18 +225,19 @@
     q_sel = column(0)
     for j in nearest[1:]:
         q_sel += column(j)
-    q_sel = q_sel.astype(jnp.bfloat16).reshape(blocks, rows, hd)
+    qsel_ref[...] = q_sel.astype(jnp.bfloat16).reshape(blocks, rows, hd)
 
     loads[5].wait()
     step = blocks // chunks
     position = reals((step, rows, tokens), 2)
-    outs, lses = [], []
-    for c in range(chunks):
-        part = slice(c * step, (c + 1) * step)
+
+    def attend(c):
+        part = pl.ds(c * step, step)
         scores = jnp.einsum(
-            "bqd,btd->bqt", q_sel[part], kv[part, :, :hd], preferred_element_type=jnp.float32
+            "bqd,btd->bqt", qsel_ref[part], kv[part, :, :hd], preferred_element_type=jnp.float32
         ) * scale
-        limit = jnp.broadcast_to(usable[part][:, None, :], (step, rows, 1))
+        limit = jnp.broadcast_to(limit_ref[part], (step, 1, 128))
+        limit = jnp.concatenate([limit] * (tokens // 128), axis=2)
         scores = jnp.where(position < limit, scores, masked_value)
         top = jnp.max(scores, axis=2, keepdims=True)
         weights = jnp.exp(scores - top)
@@ -215,16 +246,15 @@
             "bqt,btd->bqd", weights.astype(jnp.bfloat16), kv[part, :, hd:],
             preferred_element_type=jnp.float32,
         )
-        outs.append(out / total)
-        lses.append(jnp.sum(jnp.where(spread[None], top + jnp.log(total), 0.0), axis=1))
-    out = jnp.concatenate(outs, axis=0)
-    lse = jnp.concatenate(lses, axis=0)
+        out_blocks[part] = out / total
+        lse_ref[c] = jnp.sum(jnp.where(spread[None], top + jnp.log(total), 0.0), axis=1)
+
+    loop(0, chunks, attend)
+    out = out_blocks[...]
+    lse = lse_ref[...].reshape(blocks, 128)
 
     def o_copy(g):
         return remote(pbuf.at[g], rbuf.at[back(g)], so.at[0], ro.at[back(g) // N], near[g])
-
-    def l_copy(g):
-        return remote(lz.at[g], rl.at[back(g)], sl.at[0], rls.at[0], near[g])
 
     wanted = jnp.broadcast_to(request, (blocks, 128))
     best = lse
@@ -240,62 +270,48 @@
     slots = jnp.broadcast_to(slot, (blocks, 128))
     sub = lax.shift_right_logical(iota((blocks, 128), 1), rows.bit_length() - 1)
     for g in order + [0]:
-        lz[g] = jnp.max(
-            jnp.where(slots - g * F == sub, lse, masked_value), axis=0, keepdims=True
-        )
-        if g:
-            l_copy(g).start()
+        row = jnp.max(jnp.where(slots - g * F == sub, lse, masked_value), axis=0, keepdims=True)
+        pbuf[g, F] = in_three(row, rows)
     scaled = (out * to_column((factor / total)[:, None, :], blocks, rows)).reshape(own_rows, hd)
     high = scaled.astype(jnp.bfloat16)
     low = (scaled - high.astype(jnp.float32)).astype(jnp.bfloat16)
     both = jnp.concatenate([high, low], axis=1)
     for j in nearest[::-1]:
         put = dot(put_ref[j], both)
-        pbuf[j * N : (j + 1) * N] = (
+        pbuf[j * N : (j + 1) * N, :F] = (
             (put[:, :hd] + put[:, hd:]).astype(jnp.bfloat16).reshape(N, F, rows, hd)
         )
         for g in order:
             if g // N == j:
                 o_copy(g).start()
     rbuf[0] = pbuf[0]
-    rl[0] = lz[0]
-
-    def merged(values, count):
+
+    def merged(buf, count):
+        values = jnp.sum(buf[:, F].astype(jnp.float32), axis=1, keepdims=True)
         high = jnp.max(values, axis=0, keepdims=True)
         factor = jnp.exp(values - high)
         total = jnp.sum(factor, axis=0, keepdims=True)
-        return to_column(factor / total, count, frows), high + jnp.log(total)
-
-    arrived(rl.at[1:G], rls.at[0], sl.at[0])
-    share, lse = merged(rl[...], G + 1)
-    fl[0] = lse[0]
-    acc = jnp.zeros((frows, hd), jnp.float32)
-    acc += share[G] * rbuf[G].astype(jnp.float32).reshape(frows, hd)
+        share = to_column(factor / total, count, frows)
+        acc = share[0] * buf[0, :F].astype(jnp.float32).reshape(frows, hd)
+        for g in range(1, count):
+            acc += share[g] * buf[g, :F].astype(jnp.float32).reshape(frows, hd)
+        return acc.astype(jnp.bfloat16).reshape(F, rows, hd), high[0] + jnp.log(total[0])
+
     for j in nearest:
         group_arrived(rbuf, ro, so.at[0], j)
-        for g in range(j * N, (j + 1) * N):
-            acc += share[g] * rbuf[g].astype(jnp.float32).reshape(frows, hd)
-    fb[0] = acc.astype(jnp.bfloat16).reshape(F, rows, hd)
+    out, lse = merged(rbuf, G + 1)
+    fb[0, :F] = out
+    fb[0, F] = in_three(lse, rows)
 
     def fo_copy(j):
         return remote(fb.at[0], fb.at[F - j], sfo.at[j], rfo.at[F - j], far[j])
 
-    def fl_copy(j):
-        return remote(fl.at[0], fl.at[F - j], sfl.at[j], rfl.at[F - j], far[j])
-
-    for j in range(1, F):
-        fl_copy(j).start()
     for j in range(1, F):
         fo_copy(j).start()
     loads[6].wait()
     for j in range(1, F):
-        arrived(fl.at[j], rfl.at[j], sfl.at[0])
-    share, _ = merged(fl[...], F)
-    acc = share[0] * fb[0].astype(jnp.float32).reshape(frows, hd)
-    for j in range(1, F):
         arrived(fb.at[j], rfo.at[j], sfo.at[0])
-        acc += share[j] * fb[j].astype(jnp.float32).reshape(frows, hd)
-    abuf[0] = acc.astype(jnp.bfloat16).reshape(F, rows, hd)
+    abuf[0] = merged(fb, F)[0]
 
     def a_near(g):
         return remote(abuf.at[0], abuf.at[back(g)], sg.at[0], rg.at[back(g) // N], near[g])
@@ -306,9 +322,7 @@
     for j in range(1, F):
         q_far(j).wait_send()
         fo_copy(j).wait_send()
-        fl_copy(j).wait_send()
     all_sent(qbuf.at[1:G], sp.at[0], rp.at[0])
-    all_sent(lz.at[1:G], sl.at[0], rls.at[0])
     all_sent(pbuf.at[1:G], so.at[0], ro.at[0])
 
     def y_copy(j, u, to):
@@ -317,11 +331,10 @@
             se.at[0], re.at[0], (pool, to),
         )
 
-    for j in nearest:
+    def project(j):
         group_arrived(abuf, rg, sg.at[0], j)
         for c in range(N):
-            at = j * N + lax.rem(c + N - n, N)
-            piece = abuf[at].astype(jnp.float32)
+            piece = abuf[j * N + lax.rem(c + N - n, N)].astype(jnp.float32)
             for i in range(F):
                 att[(i * N + c) * rows : (i * N + c + 1) * rows] = piece[i]
         halves = []
@@ -331,7 +344,7 @@
         a = jnp.concatenate(halves, axis=0).astype(jnp.bfloat16)
         ysend[j] = dot(a, w[...]).reshape(2, Z, w.shape[1])
         for u in range(t_per_x):
-            to = xs[j] * t_per_x + u
+            to = lax.rem(x + j, X) * t_per_x + u
 
             @pl.when(to != ten)
             def _():
@@ -341,6 +354,8 @@
             def _():
                 fin[0] = ysend[j, :, u * per_t : (u + 1) * per_t]
 
+    project(0)
+    loop(1, X, lambda i: project(i + lax.div(i, 2) * (1 - 2 * lax.rem(i, 2))))
     all_sent(abuf.at[1:G], sg.at[0], rg.at[0])
     arrived(fin.at[1:T], re.at[0], se.at[0])
     out_ref[...] = jnp.sum(fin[...], axis=0).astype(jnp.bfloat16)
@@ -376,12 +391,15 @@
             pltpu.VMEM((G, F, rows, hd), bf16),
             pltpu.VMEM((X, own_rows, half), bf16),
             pltpu.VMEM((X, half, own_rows), bf16),
-            pltpu.VMEM((G, F, rows, hd), bf16),
-            pltpu.VMEM((G, 1, 128), f32),
-            pltpu.VMEM((G + 1, F, rows, hd), bf16),
-            pltpu.VMEM((G + 1, 1, 128), f32),
-            pltpu.VMEM((F, F, rows, hd), bf16),
-            pltpu.VMEM((F, 1, 128), f32),
+            pltpu.VMEM((own_rows, 128), i32),
+            pltpu.VMEM((1, own_rows), f32),
+            pltpu.VMEM((blocks, 1, 128), f32),
+            pltpu.VMEM((blocks, rows, hd), bf16),
+            pltpu.VMEM((blocks, rows, hd), f32),
+            pltpu.VMEM((chunks, blocks // chunks, 128), f32),
+            pltpu.VMEM((G, F + 1, rows, hd), bf16),
+            pltpu.VMEM((G + 1, F + 1, rows, hd), bf16),
+            pltpu.VMEM((F, F + 1, rows, hd), bf16),
             pltpu.VMEM((G, F, rows, hd), bf16),
             pltpu.VMEM((Z * rows, hd), f32),
             pltpu.VMEM((X, 2, Z, columns), f32),
@@ -389,20 +407,20 @@
             dma((7,)),
             dma((F,)), dma((F,)),
             dma((1,)), dma((X,)),
-            dma((1,)), dma((X,)), dma((1,)), dma((1,)),
-            dma((F,)), dma((F,)), dma((F,)), dma((F,)),
+            dma((1,)), dma((X,)),
+            dma((F,)), dma((F,)),
             dma((1,)), dma((X,)),
             dma((1,)), dma((1,)),
         ],
         compiler_params=pltpu.CompilerParams(
-            collective_id=0, has_side_effects=True, vmem_limit_bytes=60 * 1024 * 1024
+            collective_id=0, has_side_effects=True, vmem_limit_bytes=40 * 1024 * 1024
         ),
-    )(*args)
+    )(*[pltpu.with_memory_space_constraint(a, pltpu.HBM) for a in args])
 
 
 def solution(mesh):
     pools, tensors = mesh.shape["pool"], mesh.shape["tensor"]
-    Z = 16 if pools == 64 else 8
+    Z = 16
     placed = (
         P("pool", "tensor", None, None),
         P(None, "pool", "tensor", None),

time: 55.2 us -> 54 us (0.978)
  local copies, waits for them, and re-layouts: 1.28 us -> 0.6 us
    unnamed x1, local copies, waits for them, and re-layouts: 1.28 us -> 0.6 us
where the time goes in v5:
time: 54 us; the launch traced here: 53.9 us
  Pallas kernels  53.3 us (99%)
  local copies, waits for them, and re-layouts  0.6 us (1%)
    pallas_call x1, Pallas kernels, body(): pl.pallas_call(functools.partial(kernel, X, Z, T), out_shape=jax.ShapeDty...  53.3 us

profile of v5, /device:TPU:1, one launch (start us, length us, event | category | flops | bytes accessed | tf_op | source)
XLA Modules:
  0.0 53.9 jit_solution(3078177028136689602)
XLA Ops:
  0.0 53.3 %shard_map.73 = bf16[2,8,128]{2,1,0:T(8,128)(2,1)S(1)} custom-call(bf16[16,128]{1,0:T(8,128)(2,1)} %bitcast.7, bf16[2,256]{1,0:T(2,128)(2,1)} %bitcast.9, s32[1,64]{1,0:T(1,128)} %bitcast.10, s32[1,64]{1,0:T(1,128)} %bitcast.11, s32[1,1024]{1,0:T(1,128)} %bitcast.8, bf16[16,256,256]{2,1,0:T(8,128)(2,1)} %bitcast.6, bf16[1024,128]{1,0:T(8,128)(2,1)} %w_hbm.1), custom_call_target="tpu_custom_call" | custom-call | tf_op jit(solution)/shard_map/pallas_call | solution.py:384
  53.3 0.6 %copy.9 = bf16[2,8,128]{2,1,0:T(8,128)(2,1)} copy(bf16[2,8,128]{2,1,0:T(8,128)(2,1)S(1)} %shard_map.73) | data formatting | bytes 8192

commit v6 on v5

--- a/solution.py
+++ b/solution.py
@@ -138,6 +138,12 @@
     for j in range(1, F):
         q_far(j).start()
 
+    for j in range(1, F):
+        at = lax.rem(f + j, F)
+        arrived(qbuf.at[0, at], rf.at[at], sf.at[0])
+    for g in order:
+        q_near(g).start()
+
     for load in loads[1:5]:
         load.wait()
     cnt = cnt_ref[...].astype(jnp.float32)
@@ -167,34 +173,8 @@
 
     loop(0, X, fill_pick)
 
-    q_own = qbuf[0, f].astype(jnp.float32)
-    new = nk_ref[...].astype(jnp.float32)
-    score0 = jnp.sum(q_own * new[0:1, :hd], axis=1, keepdims=True) * scale
-    score1 = jnp.sum(q_own * new[1:2, :hd], axis=1, keepdims=True) * scale
-    score1 = jnp.where(iota((rows, 1), 0) >= heads, score1, masked_value)
-    new_max = jnp.maximum(score0, score1)
-    weight0, weight1 = jnp.exp(score0 - new_max), jnp.exp(score1 - new_max)
-    new_sum = weight0 + weight1
-    new_out = (
-        weight0.astype(jnp.bfloat16).astype(jnp.float32) * new[0:1, hd:]
-        + weight1.astype(jnp.bfloat16).astype(jnp.float32) * new[1:2, hd:]
-    ) / new_sum
     lane = iota((rows, 128), 1)
     spread = jnp.bitwise_and(lane, rows - 1) == iota((rows, 128), 0)
-    new_lse = jnp.sum(
-        jnp.where(spread, new_max + jnp.log(new_sum), 0.0), axis=0, keepdims=True
-    )
-    rbuf[G] = jnp.zeros((F + 1, rows, hd), jnp.bfloat16)
-    new_lse = jnp.where(lax.div(iota((1, 128), 1), rows) == f, new_lse, masked_value)
-    rbuf[G, F] = in_three(new_lse, rows)
-    rbuf[G, f] = new_out.astype(jnp.bfloat16)
-
-    for j in range(1, F):
-        at = lax.rem(f + j, F)
-        arrived(qbuf.at[0, at], rf.at[at], sf.at[0])
-    for g in order:
-        q_near(g).start()
-
     slot_lane = jnp.sum(
         jnp.where(
             lax.shift_right_logical(iota((blocks, own_rows), 1), rows.bit_length() - 1)
@@ -285,6 +265,26 @@
             if g // N == j:
                 o_copy(g).start()
     rbuf[0] = pbuf[0]
+
+    q_own = qbuf[0, f].astype(jnp.float32)
+    new = nk_ref[...].astype(jnp.float32)
+    score0 = jnp.sum(q_own * new[0:1, :hd], axis=1, keepdims=True) * scale
+    score1 = jnp.sum(q_own * new[1:2, :hd], axis=1, keepdims=True) * scale
+    score1 = jnp.where(iota((rows, 1), 0) >= heads, score1, masked_value)
+    new_max = jnp.maximum(score0, score1)
+    weight0, weight1 = jnp.exp(score0 - new_max), jnp.exp(score1 - new_max)
+    new_sum = weight0 + weight1
+    new_out = (
+        weight0.astype(jnp.bfloat16).astype(jnp.float32) * new[0:1, hd:]
+        + weight1.astype(jnp.bfloat16).astype(jnp.float32) * new[1:2, hd:]
+    ) / new_sum
+    new_lse = jnp.sum(
+        jnp.where(spread, new_max + jnp.log(new_sum), 0.0), axis=0, keepdims=True
+    )
+    rbuf[G] = jnp.zeros((F + 1, rows, hd), jnp.bfloat16)
+    new_lse = jnp.where(lax.div(iota((1, 128), 1), rows) == f, new_lse, masked_value)
+    rbuf[G, F] = in_three(new_lse, rows)
+    rbuf[G, f] = new_out.astype(jnp.bfloat16)
 
     def merged(buf, count):
         values = jnp.sum(buf[:, F].astype(jnp.float32), axis=1, keepdims=True)

time: 54 us -> 54 us (level)
  no operation moved by 1% of the time
where the time goes in v6:
time: 54 us; the launch traced here: 53.9 us
  Pallas kernels  53.3 us (99%)
  local copies, waits for them, and re-layouts  0.6 us (1%)
    pallas_call x1, Pallas kernels, body(): pl.pallas_call(functools.partial(kernel, X, Z, T), out_shape=jax.ShapeDty...  53.3 us

profile of v6, /device:TPU:1, one launch (start us, length us, event | category | flops | bytes accessed | tf_op | source)
XLA Modules:
  0.0 53.9 jit_solution(8568204714036049828)
XLA Ops:
  0.0 53.3 %shard_map.73 = bf16[2,8,128]{2,1,0:T(8,128)(2,1)S(1)} custom-call(bf16[16,128]{1,0:T(8,128)(2,1)} %bitcast.7, bf16[2,256]{1,0:T(2,128)(2,1)} %bitcast.9, s32[1,64]{1,0:T(1,128)} %bitcast.10, s32[1,64]{1,0:T(1,128)} %bitcast.11, s32[1,1024]{1,0:T(1,128)} %bitcast.8, bf16[16,256,256]{2,1,0:T(8,128)(2,1)} %bitcast.6, bf16[1024,128]{1,0:T(8,128)(2,1)} %w_hbm.1), custom_call_target="tpu_custom_call" | custom-call | tf_op jit(solution)/shard_map/pallas_call | solution.py:384
  53.3 0.6 %copy.9 = bf16[2,8,128]{2,1,0:T(8,128)(2,1)} copy(bf16[2,8,128]{2,1,0:T(8,128)(2,1)S(1)} %shard_map.73) | data formatting | bytes 8192

commit v7 on v6

--- a/solution.py
+++ b/solution.py
@@ -10,7 +10,7 @@
 MESH = pl.DeviceIdType.MESH
 masked_value = -1e30
 N = 4
-chunks = 2
+chunks = 4
 
 
 def iota(shape, axis):
@@ -57,7 +57,7 @@
     X, Z, T,
     q_hbm, nk_hbm, cnt_hbm, gap_hbm, bp_hbm, kv_hbm, w_hbm, out_ref,
     nk_ref, cnt_ref, gap_ref, bp_ref, kv, w,
-    qbuf, pick_ref, put_ref, slot_ref, goes_ref, limit_ref, qsel_ref, out_blocks, lse_ref, pbuf, rbuf, fb, abuf, att, ysend, fin,
+    qbuf, pick_ref, put_ref, slot_ref, goes_ref, limit_ref, pbuf, rbuf, fb, abuf, att, ysend, fin,
     sem_in, sf, rf, sp, rp, so, ro, sfo, rfo, sg, rg, se, re,
 ):
     pool, ten = lax.axis_index("pool"), lax.axis_index("tensor")
@@ -205,16 +205,16 @@
     q_sel = column(0)
     for j in nearest[1:]:
         q_sel += column(j)
-    qsel_ref[...] = q_sel.astype(jnp.bfloat16).reshape(blocks, rows, hd)
+    q_sel = q_sel.astype(jnp.bfloat16).reshape(blocks, rows, hd)
 
     loads[5].wait()
     step = blocks // chunks
     position = reals((step, rows, tokens), 2)
 
     def attend(c):
-        part = pl.ds(c * step, step)
+        part = slice(c * step, (c + 1) * step)
         scores = jnp.einsum(
-            "bqd,btd->bqt", qsel_ref[part], kv[part, :, :hd], preferred_element_type=jnp.float32
+            "bqd,btd->bqt", q_sel[part], kv[part, :, :hd], preferred_element_type=jnp.float32
         ) * scale
         limit = jnp.broadcast_to(limit_ref[part], (step, 1, 128))
         limit = jnp.concatenate([limit] * (tokens // 128), axis=2)
@@ -226,12 +226,9 @@
             "bqt,btd->bqd", weights.astype(jnp.bfloat16), kv[part, :, hd:],
             preferred_element_type=jnp.float32,
         )
-        out_blocks[part] = out / total
-        lse_ref[c] = jnp.sum(jnp.where(spread[None], top + jnp.log(total), 0.0), axis=1)
-
-    loop(0, chunks, attend)
-    out = out_blocks[...]
-    lse = lse_ref[...].reshape(blocks, 128)
+        return out / total, jnp.sum(jnp.where(spread[None], top + jnp.log(total), 0.0), axis=1)
+
+    out, lse = [jnp.concatenate(a, axis=0) for a in zip(*[attend(c) for c in range(chunks)])]
 
     def o_copy(g):
         return remote(pbuf.at[g], rbuf.at[back(g)], so.at[0], ro.at[back(g) // N], near[g])
@@ -249,14 +246,16 @@
     lse = best + jnp.log(total)
     slots = jnp.broadcast_to(slot, (blocks, 128))
     sub = lax.shift_right_logical(iota((blocks, 128), 1), rows.bit_length() - 1)
-    for g in order + [0]:
-        row = jnp.max(jnp.where(slots - g * F == sub, lse, masked_value), axis=0, keepdims=True)
-        pbuf[g, F] = in_three(row, rows)
     scaled = (out * to_column((factor / total)[:, None, :], blocks, rows)).reshape(own_rows, hd)
     high = scaled.astype(jnp.bfloat16)
     low = (scaled - high.astype(jnp.float32)).astype(jnp.bfloat16)
     both = jnp.concatenate([high, low], axis=1)
     for j in nearest[::-1]:
+        for g in range(j * N, (j + 1) * N):
+            row = jnp.max(
+                jnp.where(slots - g * F == sub, lse, masked_value), axis=0, keepdims=True
+            )
+            pbuf[g, F] = in_three(row, rows)
         put = dot(put_ref[j], both)
         pbuf[j * N : (j + 1) * N, :F] = (
             (put[:, :hd] + put[:, hd:]).astype(jnp.bfloat16).reshape(N, F, rows, hd)
@@ -286,22 +285,33 @@
     rbuf[G, F] = in_three(new_lse, rows)
     rbuf[G, f] = new_out.astype(jnp.bfloat16)
 
-    def merged(buf, count):
-        values = jnp.sum(buf[:, F].astype(jnp.float32), axis=1, keepdims=True)
-        high = jnp.max(values, axis=0, keepdims=True)
-        factor = jnp.exp(values - high)
-        total = jnp.sum(factor, axis=0, keepdims=True)
-        share = to_column(factor / total, count, frows)
-        acc = share[0] * buf[0, :F].astype(jnp.float32).reshape(frows, hd)
+    def joined(state, buf, first, count):
+        values = jnp.sum(buf[first : first + count, F].astype(jnp.float32), axis=1, keepdims=True)
+        high = jnp.max(values, axis=0)
+        if state is not None:
+            high = jnp.maximum(high, state[0])
+        factor = jnp.exp(values - high[None])
+        total = jnp.sum(factor, axis=0)
+        share = to_column(factor, count, frows)
+        acc = share[0] * buf[first, :F].astype(jnp.float32).reshape(frows, hd)
         for g in range(1, count):
-            acc += share[g] * buf[g, :F].astype(jnp.float32).reshape(frows, hd)
-        return acc.astype(jnp.bfloat16).reshape(F, rows, hd), high[0] + jnp.log(total[0])
-
+            acc += share[g] * buf[first + g, :F].astype(jnp.float32).reshape(frows, hd)
+        if state is not None:
+            old = jnp.exp(state[0] - high)
+            total += old * state[1]
+            acc += to_column(old[None], 1, frows)[0] * state[2]
+        return high, total, acc
+
+    def settled(state):
+        out = state[2] * to_column(1.0 / state[1][None], 1, frows)[0]
+        return out.astype(jnp.bfloat16).reshape(F, rows, hd)
+
+    state = joined(None, rbuf, G, 1)
     for j in nearest:
         group_arrived(rbuf, ro, so.at[0], j)
-    out, lse = merged(rbuf, G + 1)
-    fb[0, :F] = out
-    fb[0, F] = in_three(lse, rows)
+        state = joined(state, rbuf, j * N, N)
+    fb[0, F] = in_three(state[0] + jnp.log(state[1]), rows)
+    fb[0, :F] = settled(state)
 
     def fo_copy(j):
         return remote(fb.at[0], fb.at[F - j], sfo.at[j], rfo.at[F - j], far[j])
@@ -309,9 +319,11 @@
     for j in range(1, F):
         fo_copy(j).start()
     loads[6].wait()
-    for j in range(1, F):
+    state = joined(None, fb, 0, 1)
+    for j in (1, 3, 2):
         arrived(fb.at[j], rfo.at[j], sfo.at[0])
-    abuf[0] = merged(fb, F)[0]
+        state = joined(state, fb, j, 1)
+    abuf[0] = settled(state)
 
     def a_near(g):
         return remote(abuf.at[0], abuf.at[back(g)], sg.at[0], rg.at[back(g) // N], near[g])
@@ -394,9 +406,6 @@
             pltpu.VMEM((own_rows, 128), i32),
             pltpu.VMEM((1, own_rows), f32),
             pltpu.VMEM((blocks, 1, 128), f32),
-            pltpu.VMEM((blocks, rows, hd), bf16),
-            pltpu.VMEM((blocks, rows, hd), f32),
-            pltpu.VMEM((chunks, blocks // chunks, 128), f32),
             pltpu.VMEM((G, F + 1, rows, hd), bf16),
             pltpu.VMEM((G + 1, F + 1, rows, hd), bf16),
             pltpu.VMEM((F, F + 1, rows, hd), bf16),

time: 54 us -> 54.4 us (level)
  no operation moved by 1% of the time
where the time goes in v7:
time: 54.4 us; the launch traced here: 54.3 us
  Pallas kernels  53.7 us (99%)
  local copies, waits for them, and re-layouts  0.6 us (1%)
    pallas_call x1, Pallas kernels, body(): pl.pallas_call(functools.partial(kernel, X, Z, T), out_shape=jax.ShapeDty...  53.7 us

profile of v7, /device:TPU:1, one launch (start us, length us, event | category | flops | bytes accessed | tf_op | source)
XLA Modules:
  0.0 54.3 jit_solution(14049768778170440674)
XLA Ops:
  0.0 53.7 %shard_map.73 = bf16[2,8,128]{2,1,0:T(8,128)(2,1)S(1)} custom-call(bf16[16,128]{1,0:T(8,128)(2,1)} %bitcast.7, bf16[2,256]{1,0:T(2,128)(2,1)} %bitcast.9, s32[1,64]{1,0:T(1,128)} %bitcast.10, s32[1,64]{1,0:T(1,128)} %bitcast.11, s32[1,1024]{1,0:T(1,128)} %bitcast.8, bf16[16,256,256]{2,1,0:T(8,128)(2,1)} %bitcast.6, bf16[1024,128]{1,0:T(8,128)(2,1)} %w_hbm.1), custom_call_target="tpu_custom_call" | custom-call | tf_op jit(solution)/shard_map/pallas_call | solution.py:396
  53.7 0.6 %copy.9 = bf16[2,8,128]{2,1,0:T(8,128)(2,1)} copy(bf16[2,8,128]{2,1,0:T(8,128)(2,1)S(1)} %shard_map.73) | data formatting | bytes 8192
